TPU v7x, 256 devices: a whole 4x4x8 slice. The times are simulated.
256 devices in a mesh: ctx: 32 (over z, x_lo, core), head: 8 (over y, x_hi).
Axes of the slice: x: 4 (x_hi: 2, x_lo: 2; x = x_hi * 2 + x_lo), y: 4, z: 8, core: 2. Of those that a mesh axis runs over, the one named last changes fastest.
Arguments:
- queries: bfloat16 [4096, 12288], P('ctx', 'head'), may hold values from -65 to 65
- latent: bfloat16 [4096, 576], P('ctx'), may hold values from -5 to 5
- w_uk: bfloat16 [64, 128, 512], P('head'), may hold values from -0.75 to 0.75
- w_uv: bfloat16 [64, 512, 128], P('head'), may hold values from -1.5 to 1.5
- w_out: bfloat16 [8192, 3584], P('head'), may hold values from -0.0625 to 0.0625
- span_ids: int32 [64], P('ctx'), may hold values from 0 to 63, each once
- seq_lengths: int32 [4], replicated, may hold values from 1 to 2048, 4096 in all
Outputs:
- mixed: bfloat16 [4096, 3584], P(('ctx', 'head'))
Inputs may be any that keep to these rules, and one draw needn't show every extreme that they name: `span_ids`: each of the 64 block numbers once. `seq_lengths`: they sum to 4096; the longest is 2048.
All inputs are finite; a program needn't handle non-finite values.
Results may differ from a plain program's by a relative error of at most 0.019.
Values may be sent and summed in bfloat16 or wider, within the bound.
A program may use at most 64 MiB of HBM per device.

v0:
```python
import math

import jax
import jax.numpy as jnp
from jax import lax
from jax.sharding import PartitionSpec as P

low_score = -1e30


def segment_of(positions, seq_ends):
    return jnp.sum((seq_ends[None, :] <= positions[:, None]).astype(jnp.int32), axis=1)


def keep_state(running):
    return running


def shards(queries, latent, w_uk, w_uv, w_out, span_ids, seq_lengths):
    query_rows = queries.shape[0]
    half_rows = query_rows // 2
    head_count = w_uk.shape[0]
    nope_width = w_uk.shape[1]
    latent_width = w_uk.shape[2]
    query_width = queries.shape[1] // head_count
    seq_ends = jnp.cumsum(seq_lengths)
    local_rows = jnp.arange(query_rows, dtype=jnp.int32)
    query_pos = span_ids[local_rows // half_rows] * half_rows + local_rows % half_rows
    query_seg = segment_of(query_pos, seq_ends)
    shaped = queries.reshape(query_rows, head_count, query_width)
    query_latent = jnp.einsum(
        "thn,hnl->thl", shaped[:, :, :nope_width], w_uk, preferred_element_type=jnp.float32
    ).astype(jnp.bfloat16)
    query_rope = shaped[:, :, nope_width:]
    score_scale = 1.0 / math.sqrt(query_width)
    initial = (
        jnp.full((query_rows, head_count), low_score, jnp.float32),
        jnp.zeros((query_rows, head_count), jnp.float32),
        jnp.zeros((query_rows, head_count, latent_width), jnp.float32),
    )
    key_rows = lax.all_gather(latent, "ctx", axis=0, tiled=True)
    key_pos = lax.all_gather(query_pos, "ctx", axis=0, tiled=True)
    key_count = key_rows.shape[0]
    block_rows = math.gcd(key_count, 4 * query_rows)

    def advance(block_index, state):
        block_keys = lax.dynamic_slice_in_dim(key_rows, block_index * block_rows, block_rows, 0)
        block_pos = lax.dynamic_slice_in_dim(key_pos, block_index * block_rows, block_rows, 0)
        block_seg = segment_of(block_pos, seq_ends)
        visible = (block_pos[None, :] <= query_pos[:, None]) & (
            block_seg[None, :] == query_seg[:, None]
        )

        def absorb_block(current):
            top_old, mass_old, accum_old = current
            latent_keys = block_keys[:, :latent_width]
            rope_keys = block_keys[:, latent_width:]
            scores = jnp.einsum(
                "thl,kl->thk", query_latent, latent_keys, preferred_element_type=jnp.float32
            )
            scores = (
                scores
                + jnp.einsum(
                    "thr,kr->thk", query_rope, rope_keys, preferred_element_type=jnp.float32
                )
            ) * score_scale
            scores = jnp.where(visible[:, None, :], scores, low_score)
            top_new = jnp.maximum(top_old, jnp.max(scores, axis=2))
            weights = jnp.where(visible[:, None, :], jnp.exp(scores - top_new[:, :, None]), 0.0)
            rescale = jnp.exp(top_old - top_new)
            mass_new = mass_old * rescale + jnp.sum(weights, axis=2)
            accum_new = accum_old * rescale[:, :, None] + jnp.einsum(
                "thk,kl->thl",
                weights.astype(jnp.bfloat16),
                latent_keys,
                preferred_element_type=jnp.float32,
            )
            return (top_new, mass_new, accum_new)

        return lax.cond(jnp.any(visible), absorb_block, keep_state, state)

    final = lax.fori_loop(0, key_count // block_rows, advance, initial)
    top_final, mass_final, accum_final = final
    context = (accum_final / mass_final[:, :, None]).astype(jnp.bfloat16)
    attended = jnp.einsum("thl,hlv->thv", context, w_uv, preferred_element_type=jnp.float32).astype(
        jnp.bfloat16
    )
    attended = attended.reshape(query_rows, head_count * w_uv.shape[2])
    return lax.psum_scatter(
        jnp.dot(attended, w_out, preferred_element_type=jnp.float32).astype(jnp.bfloat16),
        "head",
        scatter_dimension=0,
        tiled=True,
    )


def solution(mesh):
    return jax.shard_map(
        shards,
        mesh=mesh,
        in_specs=(
            P("ctx", "head"),
            P("ctx", None),
            P("head", None, None),
            P("head", None, None),
            P("head", None),
            P("ctx"),
            P(),
        ),
        out_specs=P(("ctx", "head"), None),
        check_vma=False,
    )
```

profile of v0, /device:TPU:1, one launch (start us, length us, event | category | flops | bytes accessed | tf_op | source)
XLA Modules:
  0.0 240.2 jit_solution(6906708804471478063)
XLA Ops:
  6.5 1.8 copy.33
  8.4 0.8 reduce-window.8
  9.2 1.2 copy.34
  10.5 0.5 fusion.15
  11.0 1.3 copy.37
  12.4 0.6 fusion.22
  13.0 1.3 fusion.29
  14.3 38.2 %all-gather = s32[32,1,128]{2,1,0:T(1,128)S(1)} all-gather(s32[1,1,128]{2,1,0:T(1,128)S(1)} %fusion.29), channel_id=1, replica_groups=mesh['ctx'=32,'head'=8] {'ctx'}, dimensions={0}, use_global_device_ids=true | all-gather | bytes 16896 | tf_op jit(solution)/shard_map/all_gather | solution.py:42
  52.5 1.3 fusion.17
  53.9 28.2 %all-gather.3.cloned.1.call-done = bf16[4096,576]{1,0:T(8,128)(2,1)} async-done(((bf16[128,576]{1,0:T(8,128)(2,1)}), bf16[4096,576]{1,0:T(8,128)(2,1)}) %all-gather.3.cloned.1.call-update) | async-done | bytes 4718608 | tf_op jit(solution)/shard_map/all_gather | solution.py:41
  82.4 72.0 %while.18 = (s32[]{:T(128)}, f32[128,8]{0,1:T(8,128)S(1)}, f32[128,8]{0,1:T(8,128)S(1)}, f32[128,8,512]{2,0,1:T(8,128)S(1)}, s32[4096]{0:T(1024)S(1)}, /*index=5...) while((s32[]{:T(128)}, f32[128,8]{0,1:T(8,128)S(1)}, ...), condition=%wide.region_9.10_spmd.clone, body=%wide.region_2.9_spmd.clone.sunk | while | flops 1147414656 | bytes 21577096 | solution.py:82
  82.4 1.3 fusion.32
  83.8 0.9 fusion.33
  85.4 6.0 %conditional.3 = ((f32[128,8]{0,1:T(8,128)S(1)}, f32[128,8]{0,1:T(8,128)S(1)}, f32[128,8,512]{2,0,1:T(8,128)S(1)})) conditional(s32[]{:T(128)} %convert_element_type.62, (f32[128,8]{0,1:T(8,128)S(1)}, f32[128,8]{0,1:T(8,128)S(1)}, f32[128,8,512]{2,0,1:T(8,128)S(1)}) %tuple.54, (pred[128,512]{0,1:T(8,128)(4,1)S(1)}, bf16[4096,576]{1,0:T(8,128)(2,1)}, ...), branch_computations={%region_5.5_spmd, %region_6.8_spmd} | conditional | flops 1147144192 | bytes 21497420 | solution.py:80
  85.4 1.4 fusion.8
  86.8 1.9 fusion.21
  88.7 0.4 fusion.3
  89.1 2.2 multiply_add_fusion
  91.4 1.3 fusion.32
  92.8 0.9 fusion.33
  94.4 6.0 %conditional.3 = ((f32[128,8]{0,1:T(8,128)S(1)}, f32[128,8]{0,1:T(8,128)S(1)}, f32[128,8,512]{2,0,1:T(8,128)S(1)})) conditional(s32[]{:T(128)} %convert_element_type.62, (f32[128,8]{0,1:T(8,128)S(1)}, f32[128,8]{0,1:T(8,128)S(1)}, f32[128,8,512]{2,0,1:T(8,128)S(1)}) %tuple.54, (pred[128,512]{0,1:T(8,128)(4,1)S(1)}, bf16[4096,576]{1,0:T(8,128)(2,1)}, ...), branch_computations={%region_5.5_spmd, %region_6.8_spmd} | conditional | flops 1147144192 | bytes 21497420 | solution.py:80
  94.4 1.4 fusion.8
  95.8 1.9 fusion.21
  98.1 2.2 multiply_add_fusion
  100.4 1.3 fusion.32
  101.8 0.9 fusion.33
  103.4 6.0 %conditional.3 = ((f32[128,8]{0,1:T(8,128)S(1)}, f32[128,8]{0,1:T(8,128)S(1)}, f32[128,8,512]{2,0,1:T(8,128)S(1)})) conditional(s32[]{:T(128)} %convert_element_type.62, (f32[128,8]{0,1:T(8,128)S(1)}, f32[128,8]{0,1:T(8,128)S(1)}, f32[128,8,512]{2,0,1:T(8,128)S(1)}) %tuple.54, (pred[128,512]{0,1:T(8,128)(4,1)S(1)}, bf16[4096,576]{1,0:T(8,128)(2,1)}, ...), branch_computations={%region_5.5_spmd, %region_6.8_spmd} | conditional | flops 1147144192 | bytes 21497420 | solution.py:80
  103.4 1.4 fusion.8
  104.8 1.9 fusion.21
  107.1 2.2 multiply_add_fusion
  109.4 1.3 fusion.32
  110.8 0.9 fusion.33
  112.4 6.0 %conditional.3 = ((f32[128,8]{0,1:T(8,128)S(1)}, f32[128,8]{0,1:T(8,128)S(1)}, f32[128,8,512]{2,0,1:T(8,128)S(1)})) conditional(s32[]{:T(128)} %convert_element_type.62, (f32[128,8]{0,1:T(8,128)S(1)}, f32[128,8]{0,1:T(8,128)S(1)}, f32[128,8,512]{2,0,1:T(8,128)S(1)}) %tuple.54, (pred[128,512]{0,1:T(8,128)(4,1)S(1)}, bf16[4096,576]{1,0:T(8,128)(2,1)}, ...), branch_computations={%region_5.5_spmd, %region_6.8_spmd} | conditional | flops 1147144192 | bytes 21497420 | solution.py:80
  112.4 1.4 fusion.8
  113.8 1.9 fusion.21
  116.1 2.2 multiply_add_fusion
  118.4 1.3 fusion.32
  119.8 0.9 fusion.33
  121.4 6.0 %conditional.3 = ((f32[128,8]{0,1:T(8,128)S(1)}, f32[128,8]{0,1:T(8,128)S(1)}, f32[128,8,512]{2,0,1:T(8,128)S(1)})) conditional(s32[]{:T(128)} %convert_element_type.62, (f32[128,8]{0,1:T(8,128)S(1)}, f32[128,8]{0,1:T(8,128)S(1)}, f32[128,8,512]{2,0,1:T(8,128)S(1)}) %tuple.54, (pred[128,512]{0,1:T(8,128)(4,1)S(1)}, bf16[4096,576]{1,0:T(8,128)(2,1)}, ...), branch_computations={%region_5.5_spmd, %region_6.8_spmd} | conditional | flops 1147144192 | bytes 21497420 | solution.py:80
  121.4 1.4 fusion.8
  122.8 1.9 fusion.21
  125.1 2.2 multiply_add_fusion
  127.4 1.3 fusion.32
  128.9 0.9 fusion.33
  130.4 6.0 %conditional.3 = ((f32[128,8]{0,1:T(8,128)S(1)}, f32[128,8]{0,1:T(8,128)S(1)}, f32[128,8,512]{2,0,1:T(8,128)S(1)})) conditional(s32[]{:T(128)} %convert_element_type.62, (f32[128,8]{0,1:T(8,128)S(1)}, f32[128,8]{0,1:T(8,128)S(1)}, f32[128,8,512]{2,0,1:T(8,128)S(1)}) %tuple.54, (pred[128,512]{0,1:T(8,128)(4,1)S(1)}, bf16[4096,576]{1,0:T(8,128)(2,1)}, ...), branch_computations={%region_5.5_spmd, %region_6.8_spmd} | conditional | flops 1147144192 | bytes 21497420 | solution.py:80
  130.4 1.4 fusion.8
  131.8 1.9 fusion.21
  134.1 2.2 multiply_add_fusion
  136.4 1.3 fusion.32
  137.9 0.9 fusion.33
  139.4 6.0 %conditional.3 = ((f32[128,8]{0,1:T(8,128)S(1)}, f32[128,8]{0,1:T(8,128)S(1)}, f32[128,8,512]{2,0,1:T(8,128)S(1)})) conditional(s32[]{:T(128)} %convert_element_type.62, (f32[128,8]{0,1:T(8,128)S(1)}, f32[128,8]{0,1:T(8,128)S(1)}, f32[128,8,512]{2,0,1:T(8,128)S(1)}) %tuple.54, (pred[128,512]{0,1:T(8,128)(4,1)S(1)}, bf16[4096,576]{1,0:T(8,128)(2,1)}, ...), branch_computations={%region_5.5_spmd, %region_6.8_spmd} | conditional | flops 1147144192 | bytes 21497420 | solution.py:80
  139.4 1.4 fusion.8
  140.8 1.9 fusion.21
  143.1 2.2 multiply_add_fusion
  145.4 1.3 fusion.32
  146.9 0.9 fusion.33
  148.4 6.0 %conditional.3 = ((f32[128,8]{0,1:T(8,128)S(1)}, f32[128,8]{0,1:T(8,128)S(1)}, f32[128,8,512]{2,0,1:T(8,128)S(1)})) conditional(s32[]{:T(128)} %convert_element_type.62, (f32[128,8]{0,1:T(8,128)S(1)}, f32[128,8]{0,1:T(8,128)S(1)}, f32[128,8,512]{2,0,1:T(8,128)S(1)}) %tuple.54, (pred[128,512]{0,1:T(8,128)(4,1)S(1)}, bf16[4096,576]{1,0:T(8,128)(2,1)}, ...), branch_computations={%region_5.5_spmd, %region_6.8_spmd} | conditional | flops 1147144192 | bytes 21497420 | solution.py:80
  148.4 1.4 fusion.8
  149.8 1.9 fusion.21
  152.1 2.2 multiply_add_fusion
  154.4 2.1 convolution_convert_fusion.2
  156.5 1.3 copy-done.2
  157.8 2.1 convolution_convert_fusion
  159.9 73.5 %reduce-scatter.2.cloned.1.call-done = bf16[16,3584]{1,0:T(8,128)(2,1)} async-done(((bf16[128,3584]{1,0:T(8,128)(2,1)}), bf16[16,3584]{1,0:T(8,128)(2,1)}) %reduce-scatter.2.cloned.1.call-update) | async-done | bytes 114704 | tf_op jit(solution)/shard_map/reduce_scatter | solution.py:89
  (77 shorter events, 4.6 us)
Async XLA Ops:
  6.5 4.0 %copy-start = (bf16[8,128,512]{2,1,0:T(8,128)(2,1)S(1)}, bf16[8,128,512]{2,1,0:T(8,128)(2,1)}, u32[]{:S(2)}) copy-start(bf16[8,128,512]{2,1,0:T(8,128)(2,1)} %param.13) | copy-start | bytes 3145732
  6.5 75.6 %all-gather.3.cloned.1.call-start = ((), (), s32[]{:S(2)}) async-start(), calls=%async_computation.1 | async-start | bytes 5406720 | tf_op jit(solution)/shard_map/all_gather | solution.py:41
  8.4 225.0 %reduce-scatter.2.cloned.1.call-start = ((), (), s32[]{:S(2)}) async-start(), calls=%async_computation.2 | async-start | bytes 1032192 | tf_op jit(solution)/shard_map/reduce_scatter | solution.py:89
  10.5 1.9 copy-start.3
  85.4 1.4 copy-start.1
  94.4 1.4 copy-start.1
  103.4 1.4 copy-start.1
  112.4 1.4 copy-start.1
  121.4 1.4 copy-start.1
  130.4 1.4 copy-start.1
  139.4 1.4 copy-start.1
  148.4 1.4 copy-start.1
  154.4 3.4 %copy-start.2 = (bf16[1024,3584]{1,0:T(8,128)(2,1)S(1)}, bf16[1024,3584]{1,0:T(8,128)(2,1)}, u32[]{:S(2)}) copy-start(bf16[1024,3584]{1,0:T(8,128)(2,1)} %param.15) | copy-start | bytes 22020100
Sparse Core Ops, SparseCore 0:
  9.2 72.8 all-gather.2
  160.0 73.2 reduce-scatter.1
where the time goes:
time: 242 us; the launch traced here: 240 us
  waiting for transfers between devices  102 us (42%)
  matrix products  48.8 us (20%)
  blocking collectives  38.2 us (16%)
  other arithmetic  24.6 us (10%)
  between operations  13.5 us (6%)
  local copies, waits for them, and re-layouts  7.29 us (3%)
  loops' own time  5.99 us (2%)
    reduce_scatter x1, waiting for transfers between devices, shards(): lax.psum_scatter(jnp.dot(attended, w_out, preferred_element_type=jnp.floa...  73.5 us
    all_gather x1, blocking collectives, shards(): key_pos = lax.all_gather(query_pos, 'ctx', axis=0, tiled=True)  38.2 us
    all_gather x1, waiting for transfers between devices, shards(): key_rows = lax.all_gather(latent, 'ctx', axis=0, tiled=True)  28.2 us
    dot_general x8, matrix products, absorb_block(): jnp.einsum('thk,kl->thl', weights.astype(jnp.bfloat16), latent_keys, pref...  18 us
    dot_general x8, matrix products, absorb_block(): jnp.einsum('thl,kl->thk', query_latent, latent_keys, preferred_element_ty...  15 us
    add x9, other arithmetic, shards(): span_ids[local_rows // half_rows] * half_rows + local_rows % half_rows  11.4 us
    dot_general x8, matrix products, absorb_block(): jnp.einsum('thr,kr->thk', query_rope, rope_keys, preferred_element_type=j...  11.2 us
    reduce_or x8, other arithmetic, advance(): return lax.cond(jnp.any(visible), absorb_block, keep_state, state)  7.21 us
  transfers between devices with their start and end apart: 2, of which 2 were waited for; matrix products, arithmetic and copies ran while one was open for 3% of the time, Pallas kernels for 0%

commit v1 on v0

v1 whole, which is shorter than its diff:
```python
import functools
import math

import jax
import jax.numpy as jnp
from jax import lax
from jax.experimental import pallas as pl
from jax.experimental.pallas import tpu as pltpu
from jax.sharding import PartitionSpec as P

MESH = pl.DeviceIdType.MESH
LOW = -1e30
F32 = jnp.float32
BF16 = jnp.bfloat16

PIECE = 96
HALF = 48
ROWS = 144


def coords():
    c = lax.axis_index("ctx")
    h = lax.axis_index("head")
    return (h % 2) * 2 + (c // 2) % 2, h // 2, c // 4, c % 2


def device(x, y, z, k):
    x = (x + 4) % 4
    y = (y + 4) % 4
    z = (z + 8) % 8
    k = k % 2
    return (z * 4 + (x % 2) * 2 + k, y * 2 + x // 2)


def gather_kernel(
    q_ref, latent_ref, w_uk_ref, ids_ref, g_ref, qk_ref, ids_out_ref, own, tags, send_sem, recv_sem, tag_send, tag_recv, local_sem
):
    x, y, z, k = coords()
    xlo = x % 2
    up = device(x, y, z + 1, k)
    down = device(x, y, z - 1, k)
    xp = device(x + 1, y, z, k)
    xm = device(x - 1, y, z, k)
    yp = device(x, y + 1, z, k)
    ym = device(x, y - 1, z, k)
    sib = device(x, y, z, k + 1)

    def block(dz, other_x=0):
        return k * 16 + ((z + dz + 8) % 8) * 2 + (xlo + other_x) % 2

    def pair(dz):
        if dz == 0:
            return pl.ds(block(0, 1), 1)
        return pl.ds(k * 16 + ((z + dz + 8) % 8) * 2, 2)

    lat = latent_ref[...]
    own[0:64, :] = lat[0:64, :512]
    rope = lat[:, 512:576].astype(F32)
    packed = jnp.concatenate([rope[0:64], rope[64:128]], axis=1).astype(BF16)
    for q in range(4):
        own[64:80, 128 * q : 128 * q + 128] = packed[16 * q : 16 * q + 16, :]
    for u in range(4):
        own[pl.ds(pl.multiple_of(80 + 16 * ((u - y + 4) % 4), 16), 16), :] = lat[64 + 16 * u : 80 + 16 * u, :512]
    row = lax.broadcasted_iota(jnp.int32, (8, 128), 1)
    tags[k, xlo, z] = jnp.where(row == 0, ids_ref[0], ids_ref[1])

    barrier = pltpu.get_barrier_semaphore()
    for d in (up, down, xp, xm, yp, ym, sib):
        pl.semaphore_signal(barrier, inc=1, device_id=d, device_id_type=MESH)
    pl.semaphore_wait(barrier, 7)

    copies = {}

    def send(name, src, dst, dev):
        n = len(copies)
        cp = pltpu.make_async_remote_copy(
            src_ref=src, dst_ref=dst, send_sem=send_sem.at[n], recv_sem=recv_sem.at[n], device_id=dev, device_id_type=MESH
        )
        cp.start()
        copies[name] = cp

    def got(name):
        copies[name].wait_recv()

    tag_copies = []

    def send_tag(ref, dev):
        n = len(tag_copies)
        cp = pltpu.make_async_remote_copy(
            src_ref=ref, dst_ref=ref, send_sem=tag_send.at[n], recv_sem=tag_recv.at[n], device_id=dev, device_id_type=MESH
        )
        cp.start()
        tag_copies.append(cp)
        return cp

    def tag(dz):
        return tags.at[k, xlo, (z + dz + 8) % 8]

    first = pl.ds(0, PIECE)
    lo = pl.ds(0, HALF)
    hi = pl.ds(HALF, HALF)

    def fwd(name, dz, dev, rows=first, other_x=0):
        ref = g_ref.at[block(dz, other_x), rows]
        send(name, ref, ref, dev)

    g0 = block(0)
    send("zu1", own.at[first], g_ref.at[g0, first], up)
    send("zd1", own.at[first], g_ref.at[g0, first], down)
    send("xm0", own.at[lo], g_ref.at[g0, lo], xp)
    send("xp0", own.at[hi], g_ref.at[g0, hi], xm)
    send("s0", own, g_ref.at[g0], sib)
    local = pltpu.make_async_copy(own, g_ref.at[g0], local_sem)
    local.start()
    tu = send_tag(tag(0), up)
    td = send_tag(tag(0), down)

    def queries(h):
        qn = q_ref[:, 192 * h : 192 * h + 128]
        qr = q_ref[:, 192 * h + 128 : 192 * h + 192].astype(F32)
        qa = jnp.dot(qn, w_uk_ref[h], preferred_element_type=F32).astype(BF16)
        qr = jnp.concatenate([qr, qr], axis=1).astype(BF16)
        for s in range(2):
            qk_ref[s, 64 * h : 64 * h + 64, 0:512] = qa[64 * s : 64 * s + 64]
            qk_ref[s, 64 * h : 64 * h + 64, 512:640] = qr[64 * s : 64 * s + 64]

    for h in range(8):
        queries(h)

    def y_out(dz):
        src = g_ref.at[pair(dz), pl.ds(80, 16)]
        send(f"ym{dz}", src, g_ref.at[pair(dz), pl.ds(128, 16)], yp)
        send(f"yp{dz}", src, g_ref.at[pair(dz), pl.ds(96, 16)], ym)

    def y_relay(dz):
        if dz <= 0:
            got(f"ym{dz}")
            send(f"yr{dz}", g_ref.at[pair(dz), pl.ds(128, 16)], g_ref.at[pair(dz), pl.ds(112, 16)], yp)
        else:
            got(f"yp{dz}")
            send(f"yr{dz}", g_ref.at[pair(dz), pl.ds(96, 16)], g_ref.at[pair(dz), pl.ds(112, 16)], ym)

    def y_done(dz):
        got(f"yp{dz}" if dz <= 0 else f"ym{dz}")
        got(f"yr{dz}")
        ref = g_ref.at[pair(dz), pl.ds(96, 48)]
        send(f"sy{dz}", ref, ref, sib)

    def z_step(n):
        if n < 4:
            got(f"zu{n}")
            if n < 3:
                fwd(f"zu{n + 1}", -n, up)
            else:
                fwd("zu4", -n, up, lo)
            fwd(f"xm{n}", -n, xp)
            got(f"zd{n}")
            if n < 3:
                fwd(f"zd{n + 1}", n, down)
            else:
                fwd("zd4", n, down, hi)
            fwd(f"xp{n}", n, xm)
            fwd(f"s{-n}", -n, sib)
            fwd(f"s{n}", n, sib)
        else:
            got("zu4")
            fwd("xm4", 4, xp, lo)
            got("zd4")
            fwd("xp4", 4, xm, hi)
            fwd("s4", 4, sib)

    def x_step(n):
        if n in (0, 4):
            got(f"xm{n}")
            got(f"xp{n}")
            y_out(n)
            fwd(f"sx{n}", n, sib, first, 1)
        else:
            got(f"xm{n}")
            y_out(-n)
            got(f"xp{n}")
            y_out(n)
            fwd(f"sx{-n}", -n, sib, first, 1)
            fwd(f"sx{n}", n, sib, first, 1)

    def tag_step(n):
        nonlocal tu, td
        tu.wait_recv()
        if n < 4:
            tu = send_tag(tag(-n), up)
            td.wait_recv()
            if n < 3:
                td = send_tag(tag(n), down)

    z_step(1)
    tag_step(1)
    local.wait()
    x_step(0)
    z_step(2)
    tag_step(2)
    x_step(1)
    y_relay(0)
    z_step(3)
    tag_step(3)
    x_step(2)
    y_relay(-1)
    y_relay(1)
    y_done(0)
    z_step(4)
    tag_step(4)
    tx = send_tag(tags.at[k, xlo], xp)
    x_step(3)
    y_relay(-2)
    y_relay(2)
    y_done(-1)
    y_done(1)
    x_step(4)
    tx.wait_recv()
    ts = send_tag(tags.at[k], sib)
    y_relay(-3)
    y_relay(3)
    y_done(-2)
    y_done(2)
    y_relay(4)
    y_done(-3)
    y_done(3)
    y_done(4)
    ts.wait_recv()
    for c in range(32):
        ids_out_ref[c : c + 1, :] = tags[c // 16, (c // 8) % 2, c % 8, 0:1, :]
    for dz in (0, -1, 1, -2, 2, -3, 3, 4):
        got(f"s{dz}")
        got(f"sx{dz}")
    for dz in (0, -1, 1, -2, 2, -3, 3, 4):
        got(f"sy{dz}")
    for cp in copies.values():
        cp.wait_send()
    for cp in tag_copies:
        cp.wait_send()


def gather(queries, latent, w_uk, span_ids):
    vmem = pl.BlockSpec(memory_space=pltpu.VMEM)
    return pl.pallas_call(
        gather_kernel,
        name="gather",
        out_shape=(
            jax.ShapeDtypeStruct((32, ROWS, 512), BF16),
            jax.ShapeDtypeStruct((2, 512, 640), BF16),
            jax.ShapeDtypeStruct((32, 128), jnp.int32),
        ),
        in_specs=[vmem, vmem, vmem, pl.BlockSpec(memory_space=pltpu.SMEM)],
        out_specs=(vmem, vmem, vmem),
        scratch_shapes=[
            pltpu.VMEM((ROWS, 512), BF16),
            pltpu.VMEM((2, 2, 8, 8, 128), jnp.int32),
            pltpu.SemaphoreType.DMA((72,)),
            pltpu.SemaphoreType.DMA((72,)),
            pltpu.SemaphoreType.DMA((9,)),
            pltpu.SemaphoreType.DMA((9,)),
            pltpu.SemaphoreType.DMA,
        ],
        compiler_params=pltpu.CompilerParams(collective_id=1, has_side_effects=True, vmem_limit_bytes=24 << 20),
    )(queries, latent, w_uk, span_ids)


GROUP = 4
KEYS = 64 * GROUP


def attend_kernel(scale, ids_ref, my_ref, len_ref, g_ref, qk_ref, w_uv_ref, out_ref, where_ref, kbuf, acc, ctx):
    y = lax.axis_index("head") // 2
    for c in range(32):
        for s in range(2):
            where_ref[ids_ref[c, s]] = 2 * ((c // 16) * 16 + (c % 8) * 2 + (c // 8) % 2) + s
    ends = []
    total = 0
    for j in range(4):
        total = total + len_ref[j]
        ends.append(total)
    log2e = scale * math.log2(math.e)
    lane = lax.broadcasted_iota(jnp.int32, (64, 128), 1)
    col = lax.broadcasted_iota(jnp.int32, (1, KEYS), 1)
    tok = lax.broadcasted_iota(jnp.int32, (64, 1), 0)

    for s in range(2):
        i = my_ref[s]
        pos_q = i * 64 + tok
        start_q = jnp.zeros((64, 1), jnp.int32)
        first = jnp.int32(0)
        for e in ends[:3]:
            start_q = jnp.where(pos_q >= e, e, start_q)
            first = jnp.where(i * 64 >= e, e, first)
        j_low = first // 64
        groups = (i - j_low) // GROUP + 1

        def step(m, carry):
            top, mass = carry
            base = i - GROUP * m
            pos_k = jnp.zeros((1, KEYS), jnp.int32)
            for u in range(GROUP):
                j = base - u
                place = where_ref[jnp.maximum(j, 0)]
                b = place // 2
                half = place % 2
                turn = y * half
                row = pl.multiple_of(80 * half, 16)
                kbuf[64 * u : 64 * u + 64, 0:512] = g_ref[b, pl.ds(row, 64), :]
                for p in range(4):
                    tile = g_ref[b, 64:80, pl.ds(pl.multiple_of(128 * ((p + turn) % 4), 128), 128)]
                    kbuf[64 * u + 16 * p : 64 * u + 16 * p + 16, 512:640] = jnp.where(
                        lane[0:16] // 64 == half, tile, jnp.zeros_like(tile)
                    )
                off = col - 64 * u
                off = (off + 16 * turn) % 64
                pos_k = jnp.where(col // 64 == u, j * 64 + off, pos_k)
            bias = jnp.where((pos_k <= pos_q) & (pos_k >= start_q), 0.0, LOW).astype(F32)
            keys = kbuf[...]
            sc = lax.dot_general(qk_ref[s], keys, (((1,), (1,)), ((), ())), preferred_element_type=F32)
            sc = (sc.reshape(8, 64, KEYS) + bias[None]).reshape(512, KEYS)
            top_new = jnp.maximum(top, jnp.max(sc, axis=1, keepdims=True))
            w = jnp.exp2((sc - top_new) * log2e)
            fade = jnp.exp2((top - top_new) * log2e)
            mass = mass * fade + w[:, 0:128] + w[:, 128:256]
            acc[...] = acc[...] * fade + jnp.dot(w.astype(BF16), keys[:, 0:512], preferred_element_type=F32)
            return top_new, mass

        acc[...] = jnp.zeros_like(acc)
        top, mass = lax.fori_loop(
            0, groups, step, (jnp.full((512, 1), LOW, F32), jnp.zeros((512, 128), F32))
        )
        total_mass = jnp.sum(mass, axis=1, keepdims=True)
        done = (acc[...] / total_mass).astype(BF16)
        for h in range(8):
            ctx[h, 64 * s : 64 * s + 64, :] = done[64 * h : 64 * h + 64]

    for h in range(8):
        out_ref[:, 128 * h : 128 * h + 128] = jnp.dot(ctx[h], w_uv_ref[h], preferred_element_type=F32).astype(BF16)


def attend(ids, span_ids, seq_lengths, g, qk, w_uv, scale):
    vmem = pl.BlockSpec(memory_space=pltpu.VMEM)
    smem = pl.BlockSpec(memory_space=pltpu.SMEM)
    return pl.pallas_call(
        functools.partial(attend_kernel, scale),
        name="attend",
        out_shape=jax.ShapeDtypeStruct((128, 1024), BF16),
        in_specs=[smem, smem, smem, vmem, vmem, vmem],
        out_specs=vmem,
        scratch_shapes=[
            pltpu.SMEM((64,), jnp.int32),
            pltpu.VMEM((KEYS, 640), BF16),
            pltpu.VMEM((512, 512), F32),
            pltpu.VMEM((8, 128, 512), BF16),
        ],
        compiler_params=pltpu.CompilerParams(vmem_limit_bytes=24 << 20),
    )(ids, span_ids, seq_lengths, g, qk, w_uv)


CHUNK = 512


def project_kernel(att_ref, w_ref, out_ref, part, got, send_sem, recv_sem):
    x, y, z, k = coords()
    xh = x // 2
    others = [(dx, dy) for dy in (2, 1, 3, 0) for dx in (1, 0) if (dx, dy) != (0, 0)]
    peers = [device(x + 2 * dx, y + dy, z, k) for dx, dy in others]
    me = y * 2 + xh

    barrier = pltpu.get_barrier_semaphore()
    for d in peers:
        pl.semaphore_signal(barrier, inc=1, device_id=d, device_id_type=MESH)
    pl.semaphore_wait(barrier, len(peers))

    copies = []
    chunks = 3584 // CHUNK
    for c in range(chunks):
        cols = slice(CHUNK * c, CHUNK * c + CHUNK)
        part[:, cols] = jnp.dot(att_ref[...], w_ref[:, cols], preferred_element_type=F32).astype(BF16)
        for n, d in enumerate(peers):
            copy = pltpu.make_async_remote_copy(
                src_ref=part.at[pl.ds(pl.multiple_of(16 * d[1], 16), 16), pl.ds(CHUNK * c, CHUNK)],
                dst_ref=got.at[n, :, pl.ds(CHUNK * c, CHUNK)],
                send_sem=send_sem.at[c, n],
                recv_sem=recv_sem.at[c, n],
                device_id=d,
                device_id_type=MESH,
            )
            copy.start()
            copies.append(copy)
    for c in range(chunks):
        cols = slice(CHUNK * c, CHUNK * c + CHUNK)
        total = part[pl.ds(pl.multiple_of(16 * me, 16), 16), cols].astype(F32)
        for n in range(len(peers)):
            copies[c * len(peers) + n].wait_recv()
            total = total + got[n, :, cols].astype(F32)
        out_ref[:, cols] = total.astype(BF16)
    for copy in copies:
        copy.wait_send()


def project(attended, w_out):
    vmem = pl.BlockSpec(memory_space=pltpu.VMEM)
    return pl.pallas_call(
        project_kernel,
        name="project",
        out_shape=jax.ShapeDtypeStruct((16, 3584), BF16),
        in_specs=[vmem, vmem],
        out_specs=vmem,
        scratch_shapes=[
            pltpu.VMEM((128, 3584), BF16),
            pltpu.VMEM((7, 16, 3584), BF16),
            pltpu.SemaphoreType.DMA((3584 // CHUNK, 7)),
            pltpu.SemaphoreType.DMA((3584 // CHUNK, 7)),
        ],
        compiler_params=pltpu.CompilerParams(collective_id=2, has_side_effects=True, vmem_limit_bytes=24 << 20),
    )(attended, w_out)


def shards(queries, latent, w_uk, w_uv, w_out, span_ids, seq_lengths):
    scale = 1.0 / math.sqrt(queries.shape[1] // w_uk.shape[0])
    g, qk, ids = gather(queries, latent, w_uk, span_ids)
    attended = attend(ids, span_ids, seq_lengths, g, qk, w_uv, scale)
    return project(attended, w_out)


def solution(mesh):
    return jax.shard_map(
        shards,
        mesh=mesh,
        in_specs=(
            P("ctx", "head"),
            P("ctx", None),
            P("head", None, None),
            P("head", None, None),
            P("head", None),
            P("ctx"),
            P(),
        ),
        out_specs=P(("ctx", "head"), None),
        check_vma=False,
    )
```

time: 242 us -> 70.8 us (0.29)
  the two profiles are of different devices: /device:TPU:1 before, /device:TPU:32 now
where the time goes in v1:
time: 70.8 us; the launch traced here: 70.5 us
  Pallas kernels  64 us (90%)
  local copies, waits for them, and re-layouts  6.46 us (9%)
    pallas_call x1, Pallas kernels, gather(): pl.pallas_call(gather_kernel, name='gather', out_shape=(jax.ShapeDtypeStr...  35.1 us
    pallas_call x1, Pallas kernels, attend(): pl.pallas_call(functools.partial(attend_kernel, scale), name='attend', ou...  15 us
    pallas_call x1, Pallas kernels, project(): pl.pallas_call(project_kernel, name='project', out_shape=jax.ShapeDtypeSt...  14 us
    unnamed x14, local copies, waits for them, and re-layouts  6.46 us

profile of v1, /device:TPU:32, one launch (start us, length us, event | category | flops | bytes accessed | tf_op | source)
XLA Modules:
  0.0 70.5 jit_solution(15805296376939092949)
XLA Ops:
  0.0 1.1 %copy.8.latent_ref = bf16[128,576]{1,0:T(8,128)(2,1)S(1)} copy(bf16[128,576]{0,1:T(8,128)(2,1)} %param.8) | data formatting | bytes 294912 | tf_op args[1]
  1.1 0.0 copy-start.1
  1.1 1.2 %copy-done.1 = bf16[8,128,512]{2,1,0:T(8,128)(2,1)S(1)} copy-done((bf16[8,128,512]{2,1,0:T(8,128)(2,1)S(1)}, bf16[8,128,512]{2,1,0:T(8,128)(2,1)}, u32[]{:S(2)}) %copy-start.1) | copy-done | bytes 1048600
  2.3 0.0 copy-start.3
  2.3 1.0 %copy-done.3 = bf16[128,1536]{1,0:T(8,128)(2,1)S(1)} copy-done((bf16[128,1536]{1,0:T(8,128)(2,1)S(1)}, bf16[128,1536]{1,0:T(8,128)(2,1)}, u32[]{:S(2)}) %copy-start.3) | copy-done | bytes 393240
  3.3 0.0 copy-start.4
  3.3 0.7 copy-done.4
  3.9 0.0 copy-start
  3.9 35.1 %gather.1 = (bf16[32,144,512]{2,1,0:T(8,128)(2,1)S(1)}, bf16[2,512,640]{2,1,0:T(8,128)(2,1)S(1)}, s32[32,128]{1,0:T(8,128)S(1)}) custom-call(bf16[128,1536]{1,0:T(8,128)(2,1)S(1)} %copy-done.3, bf16[128,576]{1,0:T(8,128)(2,1)S(1)} %copy.8.latent_ref, bf16[8,128,512]{2,1,0:T(8,128)(2,1)S(1)} %copy-done.1, s32[2]{0:T(128)S(1)} %copy-done.4), custom_call_target="tpu_custom_call" | custom-call | tf_op jit(solution)/shard_map/gather/pallas_call | solution.py:244
  39.0 0.0 copy-start.2
  39.0 1.2 %copy-done.2 = bf16[8,512,128]{2,1,0:T(8,128)(2,1)S(1)} copy-done((bf16[8,512,128]{2,1,0:T(8,128)(2,1)S(1)}, bf16[8,512,128]{2,1,0:T(8,128)(2,1)}, u32[]{:S(2)}) %copy-start.2) | copy-done | bytes 1048600
  40.2 0.0 copy-start.5
  40.2 0.7 copy-done.5
  40.9 15.0 %attend.1.att_ref = bf16[128,1024]{1,0:T(8,128)(2,1)S(1)} custom-call(s32[32,128]{1,0:T(8,128)S(1)} %get-tuple-element.8.ids_ref, s32[2]{0:T(128)S(1)} %copy-done.4, s32[4]{0:T(128)S(1)} %copy-done.5, bf16[32,144,512]{2,1,0:T(8,128)(2,1)S(1)} %get-tuple-element.9.g_ref, bf16[2,512,640]{2,1,0:T(8,128)(2,1)S(1)} %get-tuple-element.10.qk_ref, ...), custom_call_target="tpu_custom_call" | custom-call | tf_op jit(solution)/shard_map/attend/pallas_call | solution.py:344
  55.9 0.0 copy-done
  55.9 14.0 %project.1 = bf16[16,3584]{1,0:T(8,128)(2,1)S(1)} custom-call(bf16[128,1024]{1,0:T(8,128)(2,1)S(1)} %attend.1.att_ref, bf16[1024,3584]{1,0:T(8,128)(2,1)S(1)} %copy-done), custom_call_target="tpu_custom_call" | custom-call | tf_op jit(solution)/shard_map/project/pallas_call | solution.py:404
  69.9 0.6 copy.10
Async XLA Ops:
  1.1 1.2 %copy-start.1 = (bf16[8,128,512]{2,1,0:T(8,128)(2,1)S(1)}, bf16[8,128,512]{2,1,0:T(8,128)(2,1)}, u32[]{:S(2)}) copy-start(bf16[8,128,512]{2,1,0:T(8,128)(2,1)} %w_uk_ref.1) | copy-start | bytes 3145732
  2.3 1.0 %copy-start.3 = (bf16[128,1536]{1,0:T(8,128)(2,1)S(1)}, bf16[128,1536]{1,0:T(8,128)(2,1)}, u32[]{:S(2)}) copy-start(bf16[128,1536]{1,0:T(8,128)(2,1)} %q_ref.1) | copy-start | bytes 1179652
  3.3 0.7 copy-start.4
  3.9 52.0 %copy-start = (bf16[1024,3584]{1,0:T(8,128)(2,1)S(1)}, bf16[1024,3584]{1,0:T(8,128)(2,1)}, u32[]{:S(2)}) copy-start(bf16[1024,3584]{1,0:T(8,128)(2,1)} %w_ref.1) | copy-start | bytes 22020100
  39.0 1.2 %copy-start.2 = (bf16[8,512,128]{2,1,0:T(8,128)(2,1)S(1)}, bf16[8,512,128]{2,1,0:T(8,128)(2,1)}, u32[]{:S(2)}) copy-start(bf16[8,512,128]{2,1,0:T(8,128)(2,1)} %w_uv_ref.1) | copy-start | bytes 3145732
  40.2 0.7 copy-start.5

commit v2 on v1

v2 whole, which is shorter than its diff:
```python
import functools
import math

import jax
import jax.numpy as jnp
from jax import lax
from jax.experimental import pallas as pl
from jax.experimental.pallas import tpu as pltpu
from jax.sharding import PartitionSpec as P

MESH = pl.DeviceIdType.MESH
LOW = -1e30
F32 = jnp.float32
BF16 = jnp.bfloat16

ROWS = 144


def coords():
    c = lax.axis_index("ctx")
    h = lax.axis_index("head")
    return (h % 2) * 2 + (c // 2) % 2, h // 2, c // 4, c % 2


def device(x, y, z, k):
    x = (x + 4) % 4
    y = (y + 4) % 4
    z = (z + 8) % 8
    k = k % 2
    return (z * 4 + (x % 2) * 2 + k, y * 2 + x // 2)


def in_hbm(array):
    return pltpu.with_memory_space_constraint(array, pltpu.HBM)


def gather_kernel(
    q_hbm, latent_hbm, w_uk_hbm, ids_hbm, g_ref, qk_ref, ids_out_ref,
    own, tags, q_ref, lat_ref, w_uk_ref, ids_ref, send_sem, recv_sem, tag_send, tag_recv, local_sem,
):
    x, y, z, k = coords()
    xlo = x % 2
    zs = {n: device(x, y, z + n, k) for n in (1, -1, 2, -2, 3, -3, 4)}
    up, down = zs[1], zs[-1]
    xp = device(x + 1, y, z, k)
    xm = device(x - 1, y, z, k)
    ys = {n: device(x, y + n, z, k) for n in (1, 2, 3)}
    sib = device(x, y, z, k + 1)

    barrier = pltpu.get_barrier_semaphore()
    friends = (*zs.values(), xp, xm, *ys.values(), sib)
    for d in friends:
        pl.semaphore_signal(barrier, inc=1, device_id=d, device_id_type=MESH)

    loads = []
    for n, (src, dst) in enumerate(((latent_hbm, lat_ref), (ids_hbm, ids_ref), (q_hbm, q_ref), (w_uk_hbm, w_uk_ref))):
        cp = pltpu.make_async_copy(src, dst, local_sem.at[n])
        cp.start()
        loads.append(cp)

    loads[0].wait()
    lat = lat_ref[...].T
    for q in range(4):
        own[q, 0:128, :] = lat[:, 128 * q : 128 * q + 128]
    rope = lat[:, 512:576].astype(F32)
    packed = jnp.concatenate([rope[0:64], rope[64:128]], axis=1).astype(BF16)
    for q in range(4):
        own[q, 128:144, :] = packed[16 * q : 16 * q + 16, :]
    loads[1].wait()
    col = lax.broadcasted_iota(jnp.int32, (8, 128), 1)
    tags[k, xlo, z] = jnp.where(col == 0, ids_ref[0], ids_ref[1])

    pl.semaphore_wait(barrier, len(friends))

    copies = {}

    def send(name, src, dst, dev):
        n = len(copies)
        cp = pltpu.make_async_remote_copy(
            src_ref=src, dst_ref=dst, send_sem=send_sem.at[n], recv_sem=recv_sem.at[n], device_id=dev, device_id_type=MESH
        )
        cp.start()
        copies[name] = cp

    def got(name):
        copies[name].wait_recv()

    tag_copies = []

    def send_tag(ref, dev):
        n = len(tag_copies)
        cp = pltpu.make_async_remote_copy(
            src_ref=ref, dst_ref=ref, send_sem=tag_send.at[n], recv_sem=tag_recv.at[n], device_id=dev, device_id_type=MESH
        )
        cp.start()
        tag_copies.append(cp)

    def block(dz, other_x=0):
        return k * 16 + ((z + dz + 8) % 8) * 2 + (xlo + other_x) % 2

    def whole(dz, other_x=0):
        return g_ref.at[:, block(dz, other_x)]

    def fwd(name, ref, dev):
        send(name, ref, ref, dev)

    def quarter(dz, other_x=0):
        return g_ref.at[y, block(dz, other_x)]

    def y_out(dz, other_x):
        for n in (2, 1, 3):
            fwd(f"y{n}:{dz},{other_x}", quarter(dz, other_x), ys[n])

    def y_done(dz, other_x):
        for n in (1, 3, 2):
            got(f"y{n}:{dz},{other_x}")
        fwd(f"s:{dz},{other_x}", whole(dz, other_x), sib)

    g0 = block(0)
    for n in (3, -3, 4):
        send(f"z:{-n if n < 4 else 4}", own.at[y], g_ref.at[y, g0], zs[n])
    send("z:-1", own, whole(0), up)
    send("z:1", own, whole(0), down)
    send("x0a", own.at[0:2], g_ref.at[0:2, g0], xp)
    send("x0b", own.at[2:4], g_ref.at[2:4, g0], xm)
    send("s:0,0", own, whole(0), sib)
    local = pltpu.make_async_copy(own, whole(0), local_sem.at[4])
    local.start()
    for n in (3, -3, 4, 2, -2, 1, -1):
        send_tag(tags.at[k, xlo, z], zs[n])

    loads[2].wait()
    loads[3].wait()

    def queries(h):
        qn = q_ref[:, 192 * h : 192 * h + 128]
        qr = q_ref[:, 192 * h + 128 : 192 * h + 192].astype(F32)
        qa = jnp.dot(qn, w_uk_ref[h], preferred_element_type=F32).astype(BF16)
        qr = jnp.concatenate([qr, qr], axis=1).astype(BF16)
        for s in range(2):
            qk_ref[s, 64 * h : 64 * h + 64, 0:512] = qa[64 * s : 64 * s + 64]
            qk_ref[s, 64 * h : 64 * h + 64, 512:640] = qr[64 * s : 64 * s + 64]

    for h in range(8):
        queries(h)

    got("z:-3")
    y_out(-3, 0)
    fwd("x:-3", quarter(-3), xp)
    got("z:3")
    y_out(3, 0)
    fwd("x:3", quarter(3), xm)
    got("z:4")
    y_out(4, 0)
    fwd("x4a", quarter(4).at[0:80], xp)
    fwd("x4b", quarter(4).at[80:144], xm)
    got("z:-1")
    fwd("z:-2", whole(-1), up)
    fwd("x:-1", whole(-1), xp)
    fwd("s:-1,0", whole(-1), sib)
    got("z:1")
    fwd("z:2", whole(1), down)
    fwd("x:1", whole(1), xm)
    fwd("s:1,0", whole(1), sib)
    got("x0a")
    got("x0b")
    fwd("s:0,1", whole(0, 1), sib)
    for n in range(7):
        tag_copies[n].wait_recv()
    send_tag(tags.at[k, xlo], xp)
    got("x:-3")
    y_out(-3, 1)
    got("x:3")
    y_out(3, 1)
    got("x4a")
    got("x4b")
    y_out(4, 1)
    got("z:-2")
    fwd("x:-2", whole(-2), xp)
    fwd("s:-2,0", whole(-2), sib)
    got("z:2")
    fwd("x:2", whole(2), xm)
    fwd("s:2,0", whole(2), sib)
    got("x:-1")
    fwd("s:-1,1", whole(-1, 1), sib)
    got("x:1")
    fwd("s:1,1", whole(1, 1), sib)
    tag_copies[7].wait_recv()
    send_tag(tags.at[k], sib)
    y_done(-3, 0)
    y_done(3, 0)
    y_done(4, 0)
    got("x:-2")
    fwd("s:-2,1", whole(-2, 1), sib)
    got("x:2")
    fwd("s:2,1", whole(2, 1), sib)
    y_done(-3, 1)
    y_done(3, 1)
    y_done(4, 1)
    tag_copies[8].wait_recv()
    for c in range(32):
        ids_out_ref[c : c + 1, :] = tags[c // 16, (c // 8) % 2, c % 8, 0:1, :]
    for dz in (0, -1, 1, -2, 2, -3, 3, 4):
        for other_x in range(2):
            got(f"s:{dz},{other_x}")
    local.wait()
    for cp in copies.values():
        cp.wait_send()
    for cp in tag_copies:
        cp.wait_send()


def gather(queries, latent, w_uk, span_ids):
    vmem = pl.BlockSpec(memory_space=pltpu.VMEM)
    hbm = pl.BlockSpec(memory_space=pl.ANY)
    return pl.pallas_call(
        gather_kernel,
        name="gather",
        out_shape=(
            jax.ShapeDtypeStruct((4, 32, ROWS, 128), BF16),
            jax.ShapeDtypeStruct((2, 512, 640), BF16),
            jax.ShapeDtypeStruct((32, 128), jnp.int32),
        ),
        in_specs=[hbm, hbm, hbm, hbm],
        out_specs=(vmem, vmem, vmem),
        scratch_shapes=[
            pltpu.VMEM((4, ROWS, 128), BF16),
            pltpu.VMEM((2, 2, 8, 8, 128), jnp.int32),
            pltpu.VMEM((128, 1536), BF16),
            pltpu.VMEM((576, 128), BF16),
            pltpu.VMEM((8, 128, 512), BF16),
            pltpu.SMEM((2,), jnp.int32),
            pltpu.SemaphoreType.DMA((51,)),
            pltpu.SemaphoreType.DMA((51,)),
            pltpu.SemaphoreType.DMA((9,)),
            pltpu.SemaphoreType.DMA((9,)),
            pltpu.SemaphoreType.DMA((5,)),
        ],
        compiler_params=pltpu.CompilerParams(collective_id=1, has_side_effects=True, vmem_limit_bytes=24 << 20),
    )(*map(in_hbm, (queries, latent.T, w_uk, span_ids)))


GROUP = 8
KEYS = 64 * GROUP


def attend_kernel(
    scale, ids_ref, my_hbm, len_hbm, g_ref, qk_ref, w_uv_hbm, out_ref, where_ref, my_ref, len_ref, kbuf, acc, ctx, w_uv_ref, sem
):
    loads = []
    for n, (src, dst) in enumerate(((my_hbm, my_ref), (len_hbm, len_ref), (w_uv_hbm, w_uv_ref))):
        cp = pltpu.make_async_copy(src, dst, sem.at[n])
        cp.start()
        loads.append(cp)
    for c in range(32):
        for s in range(2):
            where_ref[ids_ref[c, s]] = 2 * ((c // 16) * 16 + (c % 8) * 2 + (c // 8) % 2) + s
    loads[0].wait()
    loads[1].wait()
    ends = []
    total = 0
    for j in range(4):
        total = total + len_ref[j]
        ends.append(total)
    log2e = scale * math.log2(math.e)
    lane = lax.broadcasted_iota(jnp.int32, (16, 128), 1)
    col = lax.broadcasted_iota(jnp.int32, (1, KEYS), 1)
    tok = lax.broadcasted_iota(jnp.int32, (64, 1), 0)

    for s in range(2):
        i = my_ref[s]
        pos_q = i * 64 + tok
        start_q = jnp.zeros((64, 1), jnp.int32)
        first = jnp.int32(0)
        for e in ends[:3]:
            start_q = jnp.where(pos_q >= e, e, start_q)
            first = jnp.where(i * 64 >= e, e, first)
        j_low = first // 64
        groups = (i - j_low) // GROUP + 1

        def step(m, carry):
            top, mass = carry
            base = i - GROUP * m
            pos_k = jnp.zeros((1, KEYS), jnp.int32)
            for u in range(GROUP):
                j = base - u
                place = where_ref[jnp.maximum(j, 0)]
                b = place // 2
                half = place % 2
                row = pl.multiple_of(64 * half, 64)
                for q in range(4):
                    kbuf[64 * u : 64 * u + 64, 128 * q : 128 * q + 128] = g_ref[q, b, pl.ds(row, 64), :]
                    tile = g_ref[q, b, 128:144, :]
                    kbuf[64 * u + 16 * q : 64 * u + 16 * q + 16, 512:640] = jnp.where(
                        lane // 64 == half, tile, jnp.zeros_like(tile)
                    )
                pos_k = jnp.where(col // 64 == u, j * 64 + col % 64, pos_k)
            bias = jnp.where((pos_k <= pos_q) & (pos_k >= start_q), 0.0, LOW).astype(F32)
            keys = kbuf[...]
            sc = lax.dot_general(qk_ref[s], keys, (((1,), (1,)), ((), ())), preferred_element_type=F32)
            sc = (sc.reshape(8, 64, KEYS) + bias[None]).reshape(512, KEYS)
            top_new = jnp.maximum(top, jnp.max(sc, axis=1, keepdims=True))
            w = jnp.exp2((sc - top_new) * log2e)
            fade = jnp.exp2((top - top_new) * log2e)
            mass = mass * fade + sum(w[:, 128 * e : 128 * e + 128] for e in range(KEYS // 128))
            acc[...] = acc[...] * fade + jnp.dot(w.astype(BF16), keys[:, 0:512], preferred_element_type=F32)
            return top_new, mass

        acc[...] = jnp.zeros_like(acc)
        top, mass = lax.fori_loop(
            0, groups, step, (jnp.full((512, 1), LOW, F32), jnp.zeros((512, 128), F32))
        )
        total_mass = jnp.sum(mass, axis=1, keepdims=True)
        done = (acc[...] / total_mass).astype(BF16)
        for h in range(8):
            ctx[h, 64 * s : 64 * s + 64, :] = done[64 * h : 64 * h + 64]

    loads[2].wait()
    for h in range(8):
        out_ref[:, 128 * h : 128 * h + 128] = jnp.dot(ctx[h], w_uv_ref[h], preferred_element_type=F32).astype(BF16)


def attend(ids, span_ids, seq_lengths, g, qk, w_uv, scale):
    vmem = pl.BlockSpec(memory_space=pltpu.VMEM)
    smem = pl.BlockSpec(memory_space=pltpu.SMEM)
    hbm = pl.BlockSpec(memory_space=pl.ANY)
    return pl.pallas_call(
        functools.partial(attend_kernel, scale),
        name="attend",
        out_shape=jax.ShapeDtypeStruct((128, 1024), BF16),
        in_specs=[smem, hbm, hbm, vmem, vmem, hbm],
        out_specs=vmem,
        scratch_shapes=[
            pltpu.SMEM((64,), jnp.int32),
            pltpu.SMEM((2,), jnp.int32),
            pltpu.SMEM((4,), jnp.int32),
            pltpu.VMEM((KEYS, 640), BF16),
            pltpu.VMEM((512, 512), F32),
            pltpu.VMEM((8, 128, 512), BF16),
            pltpu.VMEM((8, 512, 128), BF16),
            pltpu.SemaphoreType.DMA((3,)),
        ],
        compiler_params=pltpu.CompilerParams(vmem_limit_bytes=24 << 20),
    )(ids, in_hbm(span_ids), in_hbm(seq_lengths), g, qk, in_hbm(w_uv))


CHUNK = 512


def project_kernel(att_ref, w_ref, out_ref, part, got, send_sem, recv_sem):
    x, y, z, k = coords()
    xh = x // 2
    others = [(dx, dy) for dy in (2, 1, 3, 0) for dx in (1, 0) if (dx, dy) != (0, 0)]
    peers = [device(x + 2 * dx, y + dy, z, k) for dx, dy in others]
    me = y * 2 + xh

    barrier = pltpu.get_barrier_semaphore()
    for d in peers:
        pl.semaphore_signal(barrier, inc=1, device_id=d, device_id_type=MESH)
    pl.semaphore_wait(barrier, len(peers))

    copies = []
    chunks = 3584 // CHUNK
    for c in range(chunks):
        cols = slice(CHUNK * c, CHUNK * c + CHUNK)
        part[:, cols] = jnp.dot(att_ref[...], w_ref[:, cols], preferred_element_type=F32).astype(BF16)
        for n, d in enumerate(peers):
            copy = pltpu.make_async_remote_copy(
                src_ref=part.at[pl.ds(pl.multiple_of(16 * d[1], 16), 16), pl.ds(CHUNK * c, CHUNK)],
                dst_ref=got.at[n, :, pl.ds(CHUNK * c, CHUNK)],
                send_sem=send_sem.at[c, n],
                recv_sem=recv_sem.at[c, n],
                device_id=d,
                device_id_type=MESH,
            )
            copy.start()
            copies.append(copy)
    for c in range(chunks):
        cols = slice(CHUNK * c, CHUNK * c + CHUNK)
        total = part[pl.ds(pl.multiple_of(16 * me, 16), 16), cols].astype(F32)
        for n in range(len(peers)):
            copies[c * len(peers) + n].wait_recv()
            total = total + got[n, :, cols].astype(F32)
        out_ref[:, cols] = total.astype(BF16)
    for copy in copies:
        copy.wait_send()


def project(attended, w_out):
    vmem = pl.BlockSpec(memory_space=pltpu.VMEM)
    return pl.pallas_call(
        project_kernel,
        name="project",
        out_shape=jax.ShapeDtypeStruct((16, 3584), BF16),
        in_specs=[vmem, vmem],
        out_specs=vmem,
        scratch_shapes=[
            pltpu.VMEM((128, 3584), BF16),
            pltpu.VMEM((7, 16, 3584), BF16),
            pltpu.SemaphoreType.DMA((3584 // CHUNK, 7)),
            pltpu.SemaphoreType.DMA((3584 // CHUNK, 7)),
        ],
        compiler_params=pltpu.CompilerParams(collective_id=2, has_side_effects=True, vmem_limit_bytes=24 << 20),
    )(attended, w_out)


def shards(queries, latent, w_uk, w_uv, w_out, span_ids, seq_lengths):
    scale = 1.0 / math.sqrt(queries.shape[1] // w_uk.shape[0])
    g, qk, ids = gather(queries, latent, w_uk, span_ids)
    attended = attend(ids, span_ids, seq_lengths, g, qk, w_uv, scale)
    return project(attended, w_out)


def solution(mesh):
    return jax.shard_map(
        shards,
        mesh=mesh,
        in_specs=(
            P("ctx", "head"),
            P("ctx", None),
            P("head", None, None),
            P("head", None, None),
            P("head", None),
            P("ctx"),
            P(),
        ),
        out_specs=P(("ctx", "head"), None),
        check_vma=False,
    )
```

time: 70.8 us -> 56.1 us (0.79)
  the two profiles are of different devices: /device:TPU:32 before, /device:TPU:1 now
where the time goes in v2:
time: 56.1 us; the launch traced here: 56 us
  Pallas kernels  55.3 us (99%)
  local copies, waits for them, and re-layouts  0.65 us (1%)
    pallas_call x1, Pallas kernels, gather(): pl.pallas_call(gather_kernel, name='gather', out_shape=(jax.ShapeDtypeStr...  31.5 us
    pallas_call x1, Pallas kernels, project(): pl.pallas_call(project_kernel, name='project', out_shape=jax.ShapeDtypeSt...  15.4 us
    pallas_call x1, Pallas kernels, attend(): pl.pallas_call(functools.partial(attend_kernel, scale), name='attend', ou...  8.34 us

profile of v2, /device:TPU:1, one launch (start us, length us, event | category | flops | bytes accessed | tf_op | source)
XLA Modules:
  0.0 56.0 jit_solution(5649558464404050764)
XLA Ops:
  0.0 0.0 copy-start
  0.0 31.5 %gather.1 = (bf16[4,32,144,128]{3,2,1,0:T(8,128)(2,1)S(1)}, bf16[2,512,640]{2,1,0:T(8,128)(2,1)S(1)}, s32[32,128]{1,0:T(8,128)S(1)}) custom-call(bf16[128,1536]{1,0:T(8,128)(2,1)} %q_hbm.1, bf16[576,128]{1,0:T(8,128)(2,1)} %bitcast.1, bf16[8,128,512]{2,1,0:T(8,128)(2,1)} %w_uk_hbm.1, s32[2]{0:T(128)} %my_hbm.1), custom_call_target="tpu_custom_call" | custom-call | tf_op jit(solution)/shard_map/gather/pallas_call | solution.py:216
  31.5 8.3 %attend.1.att_ref = bf16[128,1024]{1,0:T(8,128)(2,1)S(1)} custom-call(s32[32,128]{1,0:T(8,128)S(1)} %get-tuple-element.8.ids_ref, s32[2]{0:T(128)} %my_hbm.1, s32[4]{0:T(128)} %len_hbm.1, bf16[4,32,144,128]{3,2,1,0:T(8,128)(2,1)S(1)} %get-tuple-element.9.g_ref, bf16[2,512,640]{2,1,0:T(8,128)(2,1)S(1)} %get-tuple-element.10.qk_ref, bf16[8,512,128]{2,1,0:T(8,128)(2,1)} %w_uv_hbm.1), custom_call_target="tpu_custom_call" | custom-call | tf_op jit(solution)/shard_map/attend/pallas_call | solution.py:327
  39.9 0.0 copy-done
  39.9 15.4 %project.1 = bf16[16,3584]{1,0:T(8,128)(2,1)S(1)} custom-call(bf16[128,1024]{1,0:T(8,128)(2,1)S(1)} %attend.1.att_ref, bf16[1024,3584]{1,0:T(8,128)(2,1)S(1)} %copy-done), custom_call_target="tpu_custom_call" | custom-call | tf_op jit(solution)/shard_map/project/pallas_call | solution.py:391
  55.3 0.6 %copy.9 = bf16[16,3584]{1,0:T(8,128)(2,1)} copy(bf16[16,3584]{1,0:T(8,128)(2,1)S(1)} %project.1) | data formatting | bytes 229376
Async XLA Ops:
  0.0 39.9 %copy-start = (bf16[1024,3584]{1,0:T(8,128)(2,1)S(1)}, bf16[1024,3584]{1,0:T(8,128)(2,1)}, u32[]{:S(2)}) copy-start(bf16[1024,3584]{1,0:T(8,128)(2,1)} %w_ref.1) | copy-start | bytes 22020100

commit v3 on v2

v3 whole, which is shorter than its diff:
```python
import functools
import math

import jax
import jax.numpy as jnp
from jax import lax
from jax.experimental import pallas as pl
from jax.experimental.pallas import tpu as pltpu
from jax.sharding import PartitionSpec as P

MESH = pl.DeviceIdType.MESH
LOW = -1e30
CHUNK = 512
F32 = jnp.float32
BF16 = jnp.bfloat16

ROWS = 144


def coords():
    c = lax.axis_index("ctx")
    h = lax.axis_index("head")
    return (h % 2) * 2 + (c // 2) % 2, h // 2, c // 4, c % 2


def device(x, y, z, k):
    x = (x + 4) % 4
    y = (y + 4) % 4
    z = (z + 8) % 8
    k = k % 2
    return (z * 4 + (x % 2) * 2 + k, y * 2 + x // 2)


def in_hbm(array):
    return pltpu.with_memory_space_constraint(array, pltpu.HBM)


def fused_kernel(
    log2e, q_hbm, latent_hbm, w_uk_hbm, w_uv_hbm, w_out_hbm, ids_hbm, len_hbm, out_ref,
    g_ref, own, tags, mate, q_ref, lat_ref, w_uk_ref, w_uv_ref, w_out_ref, ids_ref, len_ref,
    qt, keys_ref, acc, top, mass, att, part, shares,
    send_sem, recv_sem, tag_send, tag_recv, share_send, share_recv, local_sem,
):
    x, y, z, k = coords()
    xlo = x % 2
    zs = {n: device(x, y, z + n, k) for n in (1, -1, 2, -2, 3, -3, 4)}
    up, down = zs[1], zs[-1]
    xp = device(x + 1, y, z, k)
    xm = device(x - 1, y, z, k)
    ys = {n: device(x, y + n, z, k) for n in (1, 2, 3)}
    sib = device(x, y, z, k + 1)
    peers = [ys[2], ys[1], ys[3]] + [device(x + 2, y + n, z, k) for n in (2, 1, 3, 0)]

    barrier = pltpu.get_barrier_semaphore()
    friends = (*zs.values(), xp, xm, sib, *peers)
    for d in friends:
        pl.semaphore_signal(barrier, inc=1, device_id=d, device_id_type=MESH)

    loads = []
    for n, (src, dst) in enumerate(
        (
            (latent_hbm, lat_ref),
            (ids_hbm, ids_ref),
            (len_hbm, len_ref),
            (q_hbm, q_ref),
            (w_uk_hbm, w_uk_ref),
            (w_uv_hbm, w_uv_ref),
            (w_out_hbm, w_out_ref),
        )
    ):
        cp = pltpu.make_async_copy(src, dst, local_sem.at[n])
        cp.start()
        loads.append(cp)

    loads[0].wait()
    lat = lat_ref[...].T
    for q in range(4):
        own[q, 0:128, :] = lat[:, 128 * q : 128 * q + 128]
    rope = lat[:, 512:576].astype(F32)
    packed = jnp.concatenate([rope[0:64], rope[64:128]], axis=1).astype(BF16)
    for q in range(4):
        own[q, 128:144, :] = packed[16 * q : 16 * q + 16, :]
    loads[1].wait()
    col = lax.broadcasted_iota(jnp.int32, (8, 128), 1)
    tags[k, xlo, z] = jnp.where(col < 64, ids_ref[0] * 64 + col, ids_ref[1] * 64 + col - 64)

    pl.semaphore_wait(barrier, len(friends))

    copies = {}

    def send(name, src, dst, dev):
        n = len(copies)
        cp = pltpu.make_async_remote_copy(
            src_ref=src, dst_ref=dst, send_sem=send_sem.at[n], recv_sem=recv_sem.at[n], device_id=dev, device_id_type=MESH
        )
        cp.start()
        copies[name] = cp

    def got(name):
        copies[name].wait_recv()

    tag_copies = []

    def send_tag(ref, dev, to=None):
        n = len(tag_copies)
        cp = pltpu.make_async_remote_copy(
            src_ref=ref, dst_ref=ref if to is None else to, send_sem=tag_send.at[n], recv_sem=tag_recv.at[n], device_id=dev, device_id_type=MESH
        )
        cp.start()
        tag_copies.append(cp)

    def place(dz, other_x=0, other_core=0):
        return (k + other_core) % 2, (xlo + other_x) % 2, (z + dz + 8) % 8

    def block(dz, other_x=0, other_core=0):
        core, xl, zz = place(dz, other_x, other_core)
        return core * 16 + zz * 2 + xl

    def whole(dz, other_x=0):
        return g_ref.at[:, block(dz, other_x)]

    def fwd(name, ref, dev):
        send(name, ref, ref, dev)

    def quarter(dz, other_x=0):
        return g_ref.at[y, block(dz, other_x)]

    def y_out(dz, other_x):
        for n in (2, 1, 3):
            fwd(f"y{n}:{dz},{other_x}", quarter(dz, other_x), ys[n])

    def y_done(dz, other_x):
        for n in (1, 3, 2):
            got(f"y{n}:{dz},{other_x}")
        fwd(f"s:{dz},{other_x}", whole(dz, other_x), sib)

    g0 = block(0)
    for n in (3, -3, 4):
        send(f"z:{-n if n < 4 else 4}", own.at[y], g_ref.at[y, g0], zs[n])
    send("x0a", own.at[0:2], g_ref.at[0:2, g0], xp)
    send("x0b", own.at[2:4], g_ref.at[2:4, g0], xm)
    send("s:0,0", own, whole(0), sib)
    for n in (3, -3, 4, 2, -2, 1, -1):
        send_tag(tags.at[k, xlo, z], zs[n])
    send_tag(tags.at[k, xlo, z], sib, mate)
    send("z:-1", own, whole(0), up)
    send("z:1", own, whole(0), down)

    loads[3].wait()
    loads[4].wait()
    for h in range(8):
        qn = q_ref[:, 192 * h : 192 * h + 128]
        qr = q_ref[:, 192 * h + 128 : 192 * h + 192].astype(F32)
        qa = jnp.dot(qn, w_uk_ref[h], preferred_element_type=F32).astype(BF16)
        qr = jnp.concatenate([qr, qr], axis=1).astype(BF16)
        qt[0:512, 128 * h : 128 * h + 128] = qa.T
        qt[512:640, 128 * h : 128 * h + 128] = qr.T

    loads[2].wait()
    pos_q = tags[k, xlo, z, 0:1, :]
    start_q = jnp.zeros((1, 128), jnp.int32)
    end = jnp.int32(0)
    for j in range(3):
        end = end + len_ref[j]
        start_q = jnp.where(pos_q >= end, end, start_q)

    acc[...] = jnp.zeros_like(acc)
    top[...] = jnp.full_like(top, LOW)
    mass[...] = jnp.zeros_like(mass)
    lane = lax.broadcasted_iota(jnp.int32, (16, 128), 1)
    row = lax.broadcasted_iota(jnp.int32, (128, 1), 0)

    def absorb(places, mine=False):
        amount = 128 * len(places)
        biases = []
        for n, p in enumerate(places):
            b = block(*p)
            for q in range(4):
                if mine and n == 0:
                    feats, tile = own[q, 0:128, :], own[q, 128:144, :]
                else:
                    feats, tile = g_ref[q, b, 0:128, :], g_ref[q, b, 128:144, :]
                keys_ref[128 * n : 128 * n + 128, 128 * q : 128 * q + 128] = feats
                zero = jnp.zeros_like(tile)
                r = 128 * n + 16 * q
                keys_ref[r : r + 16, 512:640] = jnp.where(lane < 64, tile, zero)
                keys_ref[r + 64 : r + 80, 512:640] = jnp.where(lane < 64, zero, tile)
            tag = mate if mine and n == 1 else tags.at[place(*p)]
            pos_k = jnp.where(row < 64, tag[0:1, 0:1] + row, tag[0:1, 64:65] + row - 64)
            biases.append(jnp.where((pos_k <= pos_q) & (pos_k >= start_q), 0.0, LOW).astype(F32))
        bias = jnp.concatenate(biases, axis=0)
        keys = keys_ref[0:amount, :]
        scores = jnp.dot(keys, qt[...], preferred_element_type=F32) + jnp.concatenate([bias] * 8, axis=1)
        top_old = top[...]
        top_new = jnp.maximum(top_old, jnp.max(scores, axis=0, keepdims=True))
        weights = jnp.exp2((scores - top_new) * log2e)
        fade = jnp.exp2((top_old - top_new) * log2e)
        mass[...] = mass[...] * fade + jnp.sum(weights, axis=0, keepdims=True)
        acc[...] = acc[...] * fade + lax.dot_general(
            keys[:, 0:512], weights.astype(BF16), (((0,), (0,)), ((), ())), preferred_element_type=F32
        )
        top[...] = top_new

    def absorb_both(*places):
        absorb([(dz, ox, c) for dz, ox in places for c in range(2)])

    def sib_got(*places):
        for dz, ox in places:
            got(f"s:{dz},{ox}")

    sib_got((0, 0))
    tag_copies[7].wait_recv()
    absorb([(0, 0, 0), (0, 0, 1)], mine=True)
    got("z:-3")
    y_out(-3, 0)
    fwd("x:-3", quarter(-3), xp)
    got("z:3")
    y_out(3, 0)
    fwd("x:3", quarter(3), xm)
    got("z:4")
    y_out(4, 0)
    fwd("x4a", quarter(4).at[0:80], xp)
    fwd("x4b", quarter(4).at[80:144], xm)
    got("x0a")
    got("x0b")
    fwd("s:0,1", whole(0, 1), sib)
    for n in range(7):
        tag_copies[n].wait_recv()
    send_tag(tags.at[k, xlo], xp)
    got("z:-1")
    fwd("z:-2", whole(-1), up)
    fwd("x:-1", whole(-1), xp)
    fwd("s:-1,0", whole(-1), sib)
    got("z:1")
    fwd("z:2", whole(1), down)
    fwd("x:1", whole(1), xm)
    fwd("s:1,0", whole(1), sib)
    tag_copies[8].wait_recv()
    send_tag(tags.at[k], sib)
    got("x:-3")
    y_out(-3, 1)
    got("x:3")
    y_out(3, 1)
    got("x4a")
    got("x4b")
    y_out(4, 1)
    tag_copies[9].wait_recv()
    sib_got((0, 1))
    absorb_both((0, 1))
    got("z:-2")
    fwd("x:-2", whole(-2), xp)
    fwd("s:-2,0", whole(-2), sib)
    got("z:2")
    fwd("x:2", whole(2), xm)
    fwd("s:2,0", whole(2), sib)
    got("x:-1")
    fwd("s:-1,1", whole(-1, 1), sib)
    got("x:1")
    fwd("s:1,1", whole(1, 1), sib)
    sib_got((-1, 0), (1, 0))
    absorb_both((-1, 0), (1, 0))
    y_done(-3, 0)
    y_done(3, 0)
    y_done(4, 0)
    sib_got((-2, 0), (2, 0))
    absorb_both((-2, 0), (2, 0))
    sib_got((-1, 1), (1, 1))
    absorb_both((-1, 1), (1, 1))
    y_done(-3, 1)
    y_done(3, 1)
    y_done(4, 1)
    got("x:-2")
    fwd("s:-2,1", whole(-2, 1), sib)
    got("x:2")
    fwd("s:2,1", whole(2, 1), sib)
    sib_got((-3, 0), (3, 0))
    absorb_both((-3, 0), (3, 0))
    sib_got((4, 0), (4, 1))
    absorb_both((4, 0), (4, 1))
    sib_got((-3, 1), (3, 1))
    absorb_both((-3, 1), (3, 1))
    sib_got((-2, 1), (2, 1))
    absorb_both((-2, 1), (2, 1))

    loads[5].wait()
    for h in range(8):
        cols = slice(128 * h, 128 * h + 128)
        context = (acc[:, cols] / mass[:, cols]).astype(BF16)
        att[:, cols] = lax.dot_general(
            context, w_uv_ref[h], (((0,), (0,)), ((), ())), preferred_element_type=F32
        ).astype(BF16)

    loads[6].wait()
    me = device(x, y, z, k)[1]
    chunks = 3584 // CHUNK
    sent = []
    for c in range(chunks):
        cols = slice(CHUNK * c, CHUNK * c + CHUNK)
        part[:, cols] = jnp.dot(att[...], w_out_ref[:, cols], preferred_element_type=F32).astype(BF16)
        for n, d in enumerate(peers):
            cp = pltpu.make_async_remote_copy(
                src_ref=part.at[pl.ds(pl.multiple_of(16 * d[1], 16), 16), pl.ds(CHUNK * c, CHUNK)],
                dst_ref=shares.at[n, :, pl.ds(CHUNK * c, CHUNK)],
                send_sem=share_send.at[c, n],
                recv_sem=share_recv.at[c, n],
                device_id=d,
                device_id_type=MESH,
            )
            cp.start()
            sent.append(cp)
    for cp in copies.values():
        cp.wait_send()
    for cp in tag_copies:
        cp.wait_send()
    for c in range(chunks):
        cols = slice(CHUNK * c, CHUNK * c + CHUNK)
        total = part[pl.ds(pl.multiple_of(16 * me, 16), 16), cols].astype(F32)
        for n in range(len(peers)):
            sent[c * len(peers) + n].wait_recv()
            total = total + shares[n, :, cols].astype(F32)
        out_ref[:, cols] = total.astype(BF16)
    for cp in sent:
        cp.wait_send()


def shards(queries, latent, w_uk, w_uv, w_out, span_ids, seq_lengths):
    scale = 1.0 / math.sqrt(queries.shape[1] // w_uk.shape[0])
    hbm = pl.BlockSpec(memory_space=pl.ANY)
    chunks = 3584 // CHUNK
    dma = pltpu.SemaphoreType.DMA
    return pl.pallas_call(
        functools.partial(fused_kernel, scale * math.log2(math.e)),
        name="fused",
        out_shape=jax.ShapeDtypeStruct((16, 3584), BF16),
        in_specs=[hbm] * 7,
        out_specs=pl.BlockSpec(memory_space=pltpu.VMEM),
        scratch_shapes=[
            pltpu.VMEM((4, 32, ROWS, 128), BF16),
            pltpu.VMEM((4, ROWS, 128), BF16),
            pltpu.VMEM((2, 2, 8, 8, 128), jnp.int32),
            pltpu.VMEM((8, 128), jnp.int32),
            pltpu.VMEM((128, 1536), BF16),
            pltpu.VMEM((576, 128), BF16),
            pltpu.VMEM((8, 128, 512), BF16),
            pltpu.VMEM((8, 512, 128), BF16),
            pltpu.VMEM((1024, 3584), BF16),
            pltpu.SMEM((2,), jnp.int32),
            pltpu.SMEM((4,), jnp.int32),
            pltpu.VMEM((640, 1024), BF16),
            pltpu.VMEM((512, 640), BF16),
            pltpu.VMEM((512, 1024), F32),
            pltpu.VMEM((1, 1024), F32),
            pltpu.VMEM((1, 1024), F32),
            pltpu.VMEM((128, 1024), BF16),
            pltpu.VMEM((128, 3584), BF16),
            pltpu.VMEM((7, 16, 3584), BF16),
            dma((51,)),
            dma((51,)),
            dma((10,)),
            dma((10,)),
            dma((chunks, 7)),
            dma((chunks, 7)),
            dma((7,)),
        ],
        compiler_params=pltpu.CompilerParams(collective_id=1, has_side_effects=True, vmem_limit_bytes=48 << 20),
    )(*map(in_hbm, (queries, latent.T, w_uk, w_uv, w_out, span_ids, seq_lengths)))


def solution(mesh):
    return jax.shard_map(
        shards,
        mesh=mesh,
        in_specs=(
            P("ctx", "head"),
            P("ctx", None),
            P("head", None, None),
            P("head", None, None),
            P("head", None),
            P("ctx"),
            P(),
        ),
        out_specs=P(("ctx", "head"), None),
        check_vma=False,
    )
```

time: 56.1 us -> 55.5 us (0.989)
  Pallas kernels: 55.3 us -> 54.5 us
    pallas_call x3 -> x1, Pallas kernels: 55.3 us -> 54.5 us  [shards(): pl.pallas_call(functools.partial(fused_kernel, scale * math.log2(math.e))...]
where the time goes in v3:
time: 55.5 us; the launch traced here: 55.1 us
  Pallas kernels  54.5 us (98%)
  local copies, waits for them, and re-layouts  0.65 us (1%)
    pallas_call x1, Pallas kernels, shards(): pl.pallas_call(functools.partial(fused_kernel, scale * math.log2(math.e))...  54.5 us

profile of v3, /device:TPU:1, one launch (start us, length us, event | category | flops | bytes accessed | tf_op | source)
XLA Modules:
  0.0 55.1 jit_solution(13719231525407139165)
XLA Ops:
  0.0 54.5 %fused.1 = bf16[16,3584]{1,0:T(8,128)(2,1)S(1)} custom-call(bf16[128,1536]{1,0:T(8,128)(2,1)} %q_hbm.1, bf16[576,128]{1,0:T(8,128)(2,1)} %bitcast.1, bf16[8,128,512]{2,1,0:T(8,128)(2,1)} %w_uk_hbm.1, bf16[8,512,128]{2,1,0:T(8,128)(2,1)} %w_uv_hbm.1, bf16[1024,3584]{1,0:T(8,128)(2,1)} %w_out_hbm.1, s32[2]{0:T(128)} %ids_hbm.1, s32[4]{0:T(128)} %len_hbm.1), custom_call_target="tpu_custom_call" | custom-call | tf_op jit(solution)/shard_map/fused/pallas_call | solution.py:331
  54.5 0.6 %copy.9 = bf16[16,3584]{1,0:T(8,128)(2,1)} copy(bf16[16,3584]{1,0:T(8,128)(2,1)S(1)} %fused.1) | data formatting | bytes 229376

commit v4 on v3

--- a/solution.py
+++ b/solution.py
@@ -135,16 +135,16 @@
         fwd(f"s:{dz},{other_x}", whole(dz, other_x), sib)
 
     g0 = block(0)
-    for n in (3, -3, 4):
-        send(f"z:{-n if n < 4 else 4}", own.at[y], g_ref.at[y, g0], zs[n])
-    send("x0a", own.at[0:2], g_ref.at[0:2, g0], xp)
-    send("x0b", own.at[2:4], g_ref.at[2:4, g0], xm)
-    send("s:0,0", own, whole(0), sib)
     for n in (3, -3, 4, 2, -2, 1, -1):
         send_tag(tags.at[k, xlo, z], zs[n])
     send_tag(tags.at[k, xlo, z], sib, mate)
     send("z:-1", own, whole(0), up)
     send("z:1", own, whole(0), down)
+    send("x0a", own.at[0:2], g_ref.at[0:2, g0], xp)
+    send("x0b", own.at[2:4], g_ref.at[2:4, g0], xm)
+    send("s:0,0", own, whole(0), sib)
+    for n in (3, -3, 4):
+        send(f"z:{-n if n < 4 else 4}", own.at[y], g_ref.at[y, g0], zs[n])
 
     loads[3].wait()
     loads[4].wait()
@@ -164,6 +164,10 @@
         end = end + len_ref[j]
         start_q = jnp.where(pos_q >= end, end, start_q)
 
+    token = lax.broadcasted_iota(jnp.int32, (128, 128), 1)
+    own_token = (lax.broadcasted_iota(jnp.int32, (128, 128), 0) == token).astype(F32).astype(BF16)
+    for h in range(8):
+        qt[640:768, 128 * h : 128 * h + 128] = own_token
     acc[...] = jnp.zeros_like(acc)
     top[...] = jnp.full_like(top, LOW)
     mass[...] = jnp.zeros_like(mass)
@@ -172,7 +176,6 @@
 
     def absorb(places, mine=False):
         amount = 128 * len(places)
-        biases = []
         for n, p in enumerate(places):
             b = block(*p)
             for q in range(4):
@@ -187,10 +190,10 @@
                 keys_ref[r + 64 : r + 80, 512:640] = jnp.where(lane < 64, zero, tile)
             tag = mate if mine and n == 1 else tags.at[place(*p)]
             pos_k = jnp.where(row < 64, tag[0:1, 0:1] + row, tag[0:1, 64:65] + row - 64)
-            biases.append(jnp.where((pos_k <= pos_q) & (pos_k >= start_q), 0.0, LOW).astype(F32))
-        bias = jnp.concatenate(biases, axis=0)
+            hidden = jnp.where((pos_k <= pos_q) & (pos_k >= start_q), 0.0, LOW).astype(BF16)
+            keys_ref[128 * n : 128 * n + 128, 640:768] = hidden
         keys = keys_ref[0:amount, :]
-        scores = jnp.dot(keys, qt[...], preferred_element_type=F32) + jnp.concatenate([bias] * 8, axis=1)
+        scores = jnp.dot(keys, qt[...], preferred_element_type=F32)
         top_old = top[...]
         top_new = jnp.maximum(top_old, jnp.max(scores, axis=0, keepdims=True))
         weights = jnp.exp2((scores - top_new) * log2e)
@@ -208,84 +211,86 @@
         for dz, ox in places:
             got(f"s:{dz},{ox}")
 
+    def z_far():
+        for dz, dev in ((-3, xp), (3, xm)):
+            got(f"z:{dz}")
+            y_out(dz, 0)
+            fwd(f"x:{dz}", quarter(dz), dev)
+        got("z:4")
+        y_out(4, 0)
+        fwd("x4a", quarter(4).at[0:80], xp)
+        fwd("x4b", quarter(4).at[80:144], xm)
+
+    def x_far():
+        for dz in (-3, 3):
+            got(f"x:{dz}")
+            y_out(dz, 1)
+        got("x4a")
+        got("x4b")
+        y_out(4, 1)
+
+    def z_near(n):
+        for dz, ahead, side in ((-n, up, xp), (n, down, xm)):
+            got(f"z:{dz}")
+            if n == 1:
+                fwd(f"z:{2 * dz}", whole(dz), ahead)
+            fwd(f"x:{dz}", whole(dz), side)
+            fwd(f"s:{dz},0", whole(dz), sib)
+
+    def x_near(n):
+        if n == 0:
+            got("x0a")
+            got("x0b")
+            fwd("s:0,1", whole(0, 1), sib)
+        else:
+            for dz in (-n, n):
+                got(f"x:{dz}")
+                fwd(f"s:{dz},1", whole(dz, 1), sib)
+
+    def y_far(other_x):
+        for dz in (-3, 3, 4):
+            y_done(dz, other_x)
+
+    def tags_z():
+        for n in range(7):
+            tag_copies[n].wait_recv()
+        send_tag(tags.at[k, xlo], xp)
+
+    def tags_x():
+        tag_copies[8].wait_recv()
+        send_tag(tags.at[k], sib)
+
+    def take(*places):
+        sib_got(*places)
+        absorb_both(*places)
+
     sib_got((0, 0))
     tag_copies[7].wait_recv()
     absorb([(0, 0, 0), (0, 0, 1)], mine=True)
-    got("z:-3")
-    y_out(-3, 0)
-    fwd("x:-3", quarter(-3), xp)
-    got("z:3")
-    y_out(3, 0)
-    fwd("x:3", quarter(3), xm)
-    got("z:4")
-    y_out(4, 0)
-    fwd("x4a", quarter(4).at[0:80], xp)
-    fwd("x4b", quarter(4).at[80:144], xm)
-    got("x0a")
-    got("x0b")
-    fwd("s:0,1", whole(0, 1), sib)
-    for n in range(7):
-        tag_copies[n].wait_recv()
-    send_tag(tags.at[k, xlo], xp)
-    got("z:-1")
-    fwd("z:-2", whole(-1), up)
-    fwd("x:-1", whole(-1), xp)
-    fwd("s:-1,0", whole(-1), sib)
-    got("z:1")
-    fwd("z:2", whole(1), down)
-    fwd("x:1", whole(1), xm)
-    fwd("s:1,0", whole(1), sib)
-    tag_copies[8].wait_recv()
-    send_tag(tags.at[k], sib)
-    got("x:-3")
-    y_out(-3, 1)
-    got("x:3")
-    y_out(3, 1)
-    got("x4a")
-    got("x4b")
-    y_out(4, 1)
+    x_near(0)
+    tags_z()
+    z_near(1)
+    tags_x()
     tag_copies[9].wait_recv()
-    sib_got((0, 1))
-    absorb_both((0, 1))
-    got("z:-2")
-    fwd("x:-2", whole(-2), xp)
-    fwd("s:-2,0", whole(-2), sib)
-    got("z:2")
-    fwd("x:2", whole(2), xm)
-    fwd("s:2,0", whole(2), sib)
-    got("x:-1")
-    fwd("s:-1,1", whole(-1, 1), sib)
-    got("x:1")
-    fwd("s:1,1", whole(1, 1), sib)
-    sib_got((-1, 0), (1, 0))
-    absorb_both((-1, 0), (1, 0))
-    y_done(-3, 0)
-    y_done(3, 0)
-    y_done(4, 0)
-    sib_got((-2, 0), (2, 0))
-    absorb_both((-2, 0), (2, 0))
-    sib_got((-1, 1), (1, 1))
-    absorb_both((-1, 1), (1, 1))
-    y_done(-3, 1)
-    y_done(3, 1)
-    y_done(4, 1)
-    got("x:-2")
-    fwd("s:-2,1", whole(-2, 1), sib)
-    got("x:2")
-    fwd("s:2,1", whole(2, 1), sib)
-    sib_got((-3, 0), (3, 0))
-    absorb_both((-3, 0), (3, 0))
-    sib_got((4, 0), (4, 1))
-    absorb_both((4, 0), (4, 1))
-    sib_got((-3, 1), (3, 1))
-    absorb_both((-3, 1), (3, 1))
-    sib_got((-2, 1), (2, 1))
-    absorb_both((-2, 1), (2, 1))
+    take((0, 1))
+    z_far()
+    x_near(1)
+    take((-1, 0), (1, 0))
+    z_near(2)
+    x_far()
+    take((-1, 1), (1, 1))
+    y_far(0)
+    take((-2, 0), (2, 0))
+    x_near(2)
+    take((-3, 0), (3, 0), (4, 0))
+    y_far(1)
+    take((-2, 1), (2, 1))
+    take((-3, 1), (3, 1), (4, 1))
 
     loads[5].wait()
     for h in range(8):
         cols = slice(128 * h, 128 * h + 128)
-        context = (acc[:, cols] / mass[:, cols]).astype(BF16)
+        context = (acc[:, cols] * (1.0 / mass[:, cols])).astype(BF16)
         att[:, cols] = lax.dot_general(
             context, w_uv_ref[h], (((0,), (0,)), ((), ())), preferred_element_type=F32
         ).astype(BF16)
@@ -319,8 +324,8 @@
             sent[c * len(peers) + n].wait_recv()
             total = total + shares[n, :, cols].astype(F32)
         out_ref[:, cols] = total.astype(BF16)
-    for cp in sent:
-        cp.wait_send()
+        for n in range(len(peers)):
+            sent[c * len(peers) + n].wait_send()
 
 
 def shards(queries, latent, w_uk, w_uv, w_out, span_ids, seq_lengths):
@@ -346,8 +351,8 @@
             pltpu.VMEM((1024, 3584), BF16),
             pltpu.SMEM((2,), jnp.int32),
             pltpu.SMEM((4,), jnp.int32),
-            pltpu.VMEM((640, 1024), BF16),
-            pltpu.VMEM((512, 640), BF16),
+            pltpu.VMEM((768, 1024), BF16),
+            pltpu.VMEM((768, 768), BF16),
             pltpu.VMEM((512, 1024), F32),
             pltpu.VMEM((1, 1024), F32),
             pltpu.VMEM((1, 1024), F32),

time: 55.5 us -> 54.7 us (0.986)
  no operation moved by 1% of the time
where the time goes in v4:
time: 54.7 us
  Pallas kernels  54 us (99%)
  local copies, waits for them, and re-layouts  0.65 us (1%)
    pallas_call x1, Pallas kernels, shards(): pl.pallas_call(functools.partial(fused_kernel, scale * math.log2(math.e))...  54 us

profile of v4, /device:TPU:1, one launch (start us, length us, event | category | flops | bytes accessed | tf_op | source)
XLA Modules:
  0.0 54.7 jit_solution(17206247625585972518)
XLA Ops:
  0.0 54.0 %fused.1 = bf16[16,3584]{1,0:T(8,128)(2,1)S(1)} custom-call(bf16[128,1536]{1,0:T(8,128)(2,1)} %q_hbm.1, bf16[576,128]{1,0:T(8,128)(2,1)} %bitcast.1, bf16[8,128,512]{2,1,0:T(8,128)(2,1)} %w_uk_hbm.1, bf16[8,512,128]{2,1,0:T(8,128)(2,1)} %w_uv_hbm.1, bf16[1024,3584]{1,0:T(8,128)(2,1)} %w_out_hbm.1, s32[2]{0:T(128)} %ids_hbm.1, s32[4]{0:T(128)} %len_hbm.1), custom_call_target="tpu_custom_call" | custom-call | tf_op jit(solution)/shard_map/fused/pallas_call | solution.py:336
  54.0 0.6 %copy.9 = bf16[16,3584]{1,0:T(8,128)(2,1)} copy(bf16[16,3584]{1,0:T(8,128)(2,1)S(1)} %fused.1) | data formatting | bytes 229376

commit v5 on v4

--- a/solution.py
+++ b/solution.py
@@ -10,7 +10,7 @@
 
 MESH = pl.DeviceIdType.MESH
 LOW = -1e30
-CHUNK = 512
+COLUMNS = ((0, 512), (512, 1536), (1536, 2560), (2560, 3584))
 F32 = jnp.float32
 BF16 = jnp.bfloat16
 
@@ -38,7 +38,7 @@
 def fused_kernel(
     log2e, q_hbm, latent_hbm, w_uk_hbm, w_uv_hbm, w_out_hbm, ids_hbm, len_hbm, out_ref,
     g_ref, own, tags, mate, q_ref, lat_ref, w_uk_ref, w_uv_ref, w_out_ref, ids_ref, len_ref,
-    qt, keys_ref, acc, top, mass, att, part, shares,
+    qt, keys_ref, acc, top, mass, att, part, shares, totals,
     send_sem, recv_sem, tag_send, tag_recv, share_send, share_recv, local_sem,
 ):
     x, y, z, k = coords()
@@ -148,13 +148,27 @@
 
     loads[3].wait()
     loads[4].wait()
-    for h in range(8):
-        qn = q_ref[:, 192 * h : 192 * h + 128]
-        qr = q_ref[:, 192 * h + 128 : 192 * h + 192].astype(F32)
-        qa = jnp.dot(qn, w_uk_ref[h], preferred_element_type=F32).astype(BF16)
-        qr = jnp.concatenate([qr, qr], axis=1).astype(BF16)
-        qt[0:512, 128 * h : 128 * h + 128] = qa.T
-        qt[512:640, 128 * h : 128 * h + 128] = qr.T
+
+    def half_of(rows, s):
+        return [rows[16 * o + 8 * s : 16 * o + 8 * s + 8] for o in range(8)]
+
+    spot = lax.broadcasted_iota(jnp.int32, (128, 128), 1) % 64
+    feature = lax.broadcasted_iota(jnp.int32, (128, 128), 0)
+    for pair in range(4):
+        feats, ropes = [], []
+        for h in (2 * pair, 2 * pair + 1):
+            qn = q_ref[:, 192 * h : 192 * h + 128]
+            qr = q_ref[:, 192 * h + 128 : 192 * h + 192].astype(F32)
+            feats.append(jnp.dot(qn, w_uk_ref[h], preferred_element_type=F32))
+            ropes.append(jnp.concatenate([qr, qr], axis=1))
+        for s in range(2):
+            cols = slice(512 * s + 128 * pair, 512 * s + 128 * pair + 128)
+            qa = jnp.concatenate(half_of(feats[0], s) + half_of(feats[1], s), axis=0)
+            qr = jnp.concatenate(half_of(ropes[0], s) + half_of(ropes[1], s), axis=0)
+            qt[0:512, cols] = qa.astype(BF16).T
+            qt[512:640, cols] = qr.astype(BF16).T
+            token = 16 * (spot // 8) + 8 * s + spot % 8
+            qt[640:768, cols] = (feature == token).astype(F32).astype(BF16)
 
     loads[2].wait()
     pos_q = tags[k, xlo, z, 0:1, :]
@@ -164,17 +178,13 @@
         end = end + len_ref[j]
         start_q = jnp.where(pos_q >= end, end, start_q)
 
-    token = lax.broadcasted_iota(jnp.int32, (128, 128), 1)
-    own_token = (lax.broadcasted_iota(jnp.int32, (128, 128), 0) == token).astype(F32).astype(BF16)
-    for h in range(8):
-        qt[640:768, 128 * h : 128 * h + 128] = own_token
     acc[...] = jnp.zeros_like(acc)
     top[...] = jnp.full_like(top, LOW)
     mass[...] = jnp.zeros_like(mass)
     lane = lax.broadcasted_iota(jnp.int32, (16, 128), 1)
     row = lax.broadcasted_iota(jnp.int32, (128, 1), 0)
 
-    def absorb(places, mine=False):
+    def absorb(places, mine=False, cols=slice(0, 1024)):
         amount = 128 * len(places)
         for n, p in enumerate(places):
             b = block(*p)
@@ -193,19 +203,19 @@
             hidden = jnp.where((pos_k <= pos_q) & (pos_k >= start_q), 0.0, LOW).astype(BF16)
             keys_ref[128 * n : 128 * n + 128, 640:768] = hidden
         keys = keys_ref[0:amount, :]
-        scores = jnp.dot(keys, qt[...], preferred_element_type=F32)
-        top_old = top[...]
+        scores = jnp.dot(keys, qt[:, cols], preferred_element_type=F32)
+        top_old = top[:, cols]
         top_new = jnp.maximum(top_old, jnp.max(scores, axis=0, keepdims=True))
         weights = jnp.exp2((scores - top_new) * log2e)
         fade = jnp.exp2((top_old - top_new) * log2e)
-        mass[...] = mass[...] * fade + jnp.sum(weights, axis=0, keepdims=True)
-        acc[...] = acc[...] * fade + lax.dot_general(
+        mass[:, cols] = mass[:, cols] * fade + jnp.sum(weights, axis=0, keepdims=True)
+        acc[:, cols] = acc[:, cols] * fade + lax.dot_general(
             keys[:, 0:512], weights.astype(BF16), (((0,), (0,)), ((), ())), preferred_element_type=F32
         )
-        top[...] = top_new
-
-    def absorb_both(*places):
-        absorb([(dz, ox, c) for dz, ox in places for c in range(2)])
+        top[:, cols] = top_new
+
+    def absorb_both(*places, cols=slice(0, 1024)):
+        absorb([(dz, ox, c) for dz, ox in places for c in range(2)], cols=cols)
 
     def sib_got(*places):
         for dz, ox in places:
@@ -282,56 +292,79 @@
     y_far(0)
     take((-2, 0), (2, 0))
     x_near(2)
-    take((-3, 0), (3, 0), (4, 0))
+    halves = (slice(0, 512), slice(512, 1024))
+    far = [[(dz, ox) for dz in (-3, 3, 4)] for ox in range(2)]
+    last = [(-2, 1), (2, 1)]
+    sib_got(*far[0])
+    absorb_both(*far[0], cols=halves[0])
     y_far(1)
-    take((-2, 1), (2, 1))
-    take((-3, 1), (3, 1), (4, 1))
+    absorb_both(*far[0], cols=halves[1])
+    sib_got(*last)
+    absorb_both(*last, cols=halves[0])
+    sib_got(*far[1])
+    absorb_both(*far[1], cols=halves[0])
+
+    me = device(x, y, z, k)[1]
+    sent = {}
+
+    def project(s):
+        for pair in range(4):
+            cols = slice(512 * s + 128 * pair, 512 * s + 128 * pair + 128)
+            context = (acc[:, cols] * (1.0 / mass[:, cols])).astype(BF16)
+            for n in range(2):
+                h = 2 * pair + n
+                value = lax.dot_general(context, w_uv_ref[h], (((0,), (0,)), ((), ())), preferred_element_type=F32)
+                att[64 * s : 64 * s + 64, 128 * h : 128 * h + 128] = value[64 * n : 64 * n + 64].astype(BF16)
+        for c, (begin, end) in enumerate(COLUMNS):
+            width = (end - begin) // 2
+            share = jnp.dot(att[64 * s : 64 * s + 64, :], w_out_ref[:, begin:end], preferred_element_type=F32)
+            share = share.reshape(8, 8, 2 * width)
+            share = jnp.concatenate([share[:, :, :width], share[:, :, width:]], axis=1)
+            cols = slice(begin // 2, end // 2)
+            part[s, :, cols] = share.reshape(128, width).astype(BF16)
+            for n, d in enumerate(peers):
+                cp = pltpu.make_async_remote_copy(
+                    src_ref=part.at[s, pl.ds(pl.multiple_of(16 * d[1], 16), 16), pl.ds(begin // 2, width)],
+                    dst_ref=shares.at[s, n, :, pl.ds(begin // 2, width)],
+                    send_sem=share_send.at[s, c, n],
+                    recv_sem=share_recv.at[s, c, n],
+                    device_id=d,
+                    device_id_type=MESH,
+                )
+                cp.start()
+                sent[s, c, n] = cp
+
+    def total(s, c):
+        begin, end = COLUMNS[c]
+        cols = slice(begin // 2, end // 2)
+        result = part[s, pl.ds(pl.multiple_of(16 * me, 16), 16), cols].astype(F32)
+        for n in range(len(peers)):
+            sent[s, c, n].wait_recv()
+            result = result + shares[s, n, :, cols].astype(F32)
+        for n in range(len(peers)):
+            sent[s, c, n].wait_send()
+        return jnp.concatenate([result[0:8], result[8:16]], axis=1)
 
     loads[5].wait()
-    for h in range(8):
-        cols = slice(128 * h, 128 * h + 128)
-        context = (acc[:, cols] * (1.0 / mass[:, cols])).astype(BF16)
-        att[:, cols] = lax.dot_general(
-            context, w_uv_ref[h], (((0,), (0,)), ((), ())), preferred_element_type=F32
-        ).astype(BF16)
-
     loads[6].wait()
-    me = device(x, y, z, k)[1]
-    chunks = 3584 // CHUNK
-    sent = []
-    for c in range(chunks):
-        cols = slice(CHUNK * c, CHUNK * c + CHUNK)
-        part[:, cols] = jnp.dot(att[...], w_out_ref[:, cols], preferred_element_type=F32).astype(BF16)
-        for n, d in enumerate(peers):
-            cp = pltpu.make_async_remote_copy(
-                src_ref=part.at[pl.ds(pl.multiple_of(16 * d[1], 16), 16), pl.ds(CHUNK * c, CHUNK)],
-                dst_ref=shares.at[n, :, pl.ds(CHUNK * c, CHUNK)],
-                send_sem=share_send.at[c, n],
-                recv_sem=share_recv.at[c, n],
-                device_id=d,
-                device_id_type=MESH,
-            )
-            cp.start()
-            sent.append(cp)
+    project(0)
+    absorb_both(*last, cols=halves[1])
+    absorb_both(*far[1], cols=halves[1])
+    project(1)
     for cp in copies.values():
         cp.wait_send()
     for cp in tag_copies:
         cp.wait_send()
-    for c in range(chunks):
-        cols = slice(CHUNK * c, CHUNK * c + CHUNK)
-        total = part[pl.ds(pl.multiple_of(16 * me, 16), 16), cols].astype(F32)
-        for n in range(len(peers)):
-            sent[c * len(peers) + n].wait_recv()
-            total = total + shares[n, :, cols].astype(F32)
-        out_ref[:, cols] = total.astype(BF16)
-        for n in range(len(peers)):
-            sent[c * len(peers) + n].wait_send()
+    for c, (begin, end) in enumerate(COLUMNS):
+        totals[:, begin:end] = total(0, c)
+    for c, (begin, end) in enumerate(COLUMNS):
+        out_ref[:, begin:end] = jnp.concatenate([totals[:, begin:end], total(1, c)], axis=0).astype(BF16)
 
 
 def shards(queries, latent, w_uk, w_uv, w_out, span_ids, seq_lengths):
     scale = 1.0 / math.sqrt(queries.shape[1] // w_uk.shape[0])
     hbm = pl.BlockSpec(memory_space=pl.ANY)
-    chunks = 3584 // CHUNK
+    chunks = len(COLUMNS)
     dma = pltpu.SemaphoreType.DMA
     return pl.pallas_call(
         functools.partial(fused_kernel, scale * math.log2(math.e)),
@@ -357,14 +390,15 @@
             pltpu.VMEM((1, 1024), F32),
             pltpu.VMEM((1, 1024), F32),
             pltpu.VMEM((128, 1024), BF16),
-            pltpu.VMEM((128, 3584), BF16),
-            pltpu.VMEM((7, 16, 3584), BF16),
+            pltpu.VMEM((2, 128, 1792), BF16),
+            pltpu.VMEM((2, 7, 16, 1792), BF16),
+            pltpu.VMEM((8, 3584), F32),
             dma((51,)),
             dma((51,)),
             dma((10,)),
             dma((10,)),
-            dma((chunks, 7)),
-            dma((chunks, 7)),
+            dma((2, chunks, 7)),
+            dma((2, chunks, 7)),
             dma((7,)),
         ],
         compiler_params=pltpu.CompilerParams(collective_id=1, has_side_effects=True, vmem_limit_bytes=48 << 20),

time: 54.7 us -> 53.9 us (0.985)
  Pallas kernels: 54 us -> 53.2 us
    pallas_call x1, Pallas kernels: 54 us -> 53.2 us  [shards(): pl.pallas_call(functools.partial(fused_kernel, scale * math.log2(math.e))...]
where the time goes in v5:
time: 53.9 us; the launch traced here: 53.8 us
  Pallas kernels  53.2 us (99%)
  local copies, waits for them, and re-layouts  0.65 us (1%)
    pallas_call x1, Pallas kernels, shards(): pl.pallas_call(functools.partial(fused_kernel, scale * math.log2(math.e))...  53.2 us

profile of v5, /device:TPU:1, one launch (start us, length us, event | category | flops | bytes accessed | tf_op | source)
XLA Modules:
  0.0 53.8 jit_solution(17680191048652494798)
XLA Ops:
  0.0 53.2 %fused.1 = bf16[16,3584]{1,0:T(8,128)(2,1)S(1)} custom-call(bf16[128,1536]{1,0:T(8,128)(2,1)} %q_hbm.1, bf16[576,128]{1,0:T(8,128)(2,1)} %bitcast.1, bf16[8,128,512]{2,1,0:T(8,128)(2,1)} %w_uk_hbm.1, bf16[8,512,128]{2,1,0:T(8,128)(2,1)} %w_uv_hbm.1, bf16[1024,3584]{1,0:T(8,128)(2,1)} %w_out_hbm.1, s32[2]{0:T(128)} %ids_hbm.1, s32[4]{0:T(128)} %len_hbm.1), custom_call_target="tpu_custom_call" | custom-call | tf_op jit(solution)/shard_map/fused/pallas_call | solution.py:369
  53.2 0.6 %copy.9 = bf16[16,3584]{1,0:T(8,128)(2,1)} copy(bf16[16,3584]{1,0:T(8,128)(2,1)S(1)} %fused.1) | data formatting | bytes 229376

commit v6 on v5

--- a/solution.py
+++ b/solution.py
@@ -305,7 +305,6 @@
     absorb_both(*far[1], cols=halves[0])
 
     me = device(x, y, z, k)[1]
-    sent = {}
 
     def project(s):
         for pair in range(4):
@@ -326,23 +325,23 @@
                 cp = pltpu.make_async_remote_copy(
                     src_ref=part.at[s, pl.ds(pl.multiple_of(16 * d[1], 16), 16), pl.ds(begin // 2, width)],
                     dst_ref=shares.at[s, n, :, pl.ds(begin // 2, width)],
-                    send_sem=share_send.at[s, c, n],
-                    recv_sem=share_recv.at[s, c, n],
+                    send_sem=share_send.at[s, c],
+                    recv_sem=share_recv.at[s, c],
                     device_id=d,
                     device_id_type=MESH,
                 )
                 cp.start()
-                sent[s, c, n] = cp
 
     def total(s, c):
         begin, end = COLUMNS[c]
         cols = slice(begin // 2, end // 2)
         result = part[s, pl.ds(pl.multiple_of(16 * me, 16), 16), cols].astype(F32)
+        arrived = shares.at[s, :, :, pl.ds(begin // 2, (end - begin) // 2)]
+        pltpu.make_async_copy(arrived, arrived, share_recv.at[s, c]).wait()
         for n in range(len(peers)):
-            sent[s, c, n].wait_recv()
             result = result + shares[s, n, :, cols].astype(F32)
-        for n in range(len(peers)):
-            sent[s, c, n].wait_send()
+        left = part.at[s, pl.ds(0, 16 * len(peers)), pl.ds(begin // 2, (end - begin) // 2)]
+        pltpu.make_async_copy(left, left, share_send.at[s, c]).wait()
         return jnp.concatenate([result[0:8], result[8:16]], axis=1)
 
     loads[5].wait()
@@ -397,8 +396,8 @@
             dma((51,)),
             dma((10,)),
             dma((10,)),
-            dma((2, chunks, 7)),
-            dma((2, chunks, 7)),
+            dma((2, chunks)),
+            dma((2, chunks)),
             dma((7,)),
         ],
         compiler_params=pltpu.CompilerParams(collective_id=1, has_side_effects=True, vmem_limit_bytes=48 << 20),

time: 53.9 us -> 53 us (0.983)
  Pallas kernels: 53.2 us -> 52.3 us
    pallas_call x1, Pallas kernels: 53.2 us -> 52.3 us  [shards(): pl.pallas_call(functools.partial(fused_kernel, scale * math.log2(math.e))...]
where the time goes in v6:
time: 53 us
  Pallas kernels  52.3 us (99%)
  local copies, waits for them, and re-layouts  0.65 us (1%)
    pallas_call x1, Pallas kernels, shards(): pl.pallas_call(functools.partial(fused_kernel, scale * math.log2(math.e))...  52.3 us

profile of v6, /device:TPU:1, one launch (start us, length us, event | category | flops | bytes accessed | tf_op | source)
XLA Modules:
  0.0 53.0 jit_solution(6639823400230210815)
XLA Ops:
  0.0 52.3 %fused.1 = bf16[16,3584]{1,0:T(8,128)(2,1)S(1)} custom-call(bf16[128,1536]{1,0:T(8,128)(2,1)} %q_hbm.1, bf16[576,128]{1,0:T(8,128)(2,1)} %bitcast.1, bf16[8,128,512]{2,1,0:T(8,128)(2,1)} %w_uk_hbm.1, bf16[8,512,128]{2,1,0:T(8,128)(2,1)} %w_uv_hbm.1, bf16[1024,3584]{1,0:T(8,128)(2,1)} %w_out_hbm.1, s32[2]{0:T(128)} %ids_hbm.1, s32[4]{0:T(128)} %len_hbm.1), custom_call_target="tpu_custom_call" | custom-call | tf_op jit(solution)/shard_map/fused/pallas_call | solution.py:368
  52.3 0.6 %copy.9 = bf16[16,3584]{1,0:T(8,128)(2,1)} copy(bf16[16,3584]{1,0:T(8,128)(2,1)S(1)} %fused.1) | data formatting | bytes 229376
